TPU v7x, 128 devices: a whole 4x4x4 slice. The times are simulated.
128 devices in a mesh: pipe: 2 (over x_hi), dp: 32 (over z, y, x_lo), tensor: 2 (over core).
Axes of the slice: x: 4 (x_hi: 2, x_lo: 2; x = x_hi * 2 + x_lo), y: 4, z: 4, core: 2. Of those that a mesh axis runs over, the one named last changes fastest.
Arguments:
- hidden_in: bfloat16 [1, 4096, 8192], P(None, 'dp', 'tensor'), may hold values from -3 to 3
- norm_gain: float32 [2, 8192], P('pipe'), may hold values from 0.1 to 1.9
- qkv_weight: bfloat16 [2, 8192, 5120], P('pipe', None, 'tensor'), may hold values from -0.0625 to 0.0625
- qkv_bias: float32 [2, 5120], P('pipe', 'tensor'), may hold values from -3 to 3
- out_weight: bfloat16 [2, 4096, 8192], P('pipe', 'tensor', 'dp'), may hold values from -0.375 to 0.375
- segment_ids: int32 [1, 4096], P(None, 'dp'), may hold values from 0 to 1, as said below
- image_start: int32 [1, 64], P(None, 'dp'), may hold values from 1 to 124, as said below
- image_height: int32 [1, 64], P(None, 'dp'), may hold values from 2 to 6
- image_width: int32 [1, 64], P(None, 'dp'), may hold values from 2 to 6
- image_count: int32 [1, 64], P(None, 'dp'), may hold values from 0 to 1
Outputs:
- phase_outputs: bfloat16 [2, 1, 4096, 8192], P('pipe', None, 'dp', 'tensor')
Inputs may be any that keep to these rules, and one draw needn't show every extreme that they name: `segment_ids`: each stream's micro-batch of 128 tokens packs two sequences, ids 0 then 1, each of 40 tokens or more. `image_start`: the image's tokens, height times width of them row by row from this offset, lie inside its sequence and after the sequence's first token, also where image_count is 0.
All inputs are finite; a program needn't handle non-finite values.
Results may differ from a plain program's by a relative error of at most 0.013.
Values may be sent and summed in bfloat16 or wider, within the bound.
A program may use at most 192 MiB of HBM per device.

v0:
```python
import math

import jax
import jax.numpy as jnp
from jax import lax
from jax.sharding import PartitionSpec as P

HD = 128


rope_theta = 1000000.0
epsilon = 1e-06


def shifted_2(block, axis, distance):
    devices = range(lax.axis_size(axis))
    route = [(i - distance, i) for i in devices if i - distance in devices]
    return lax.ppermute(block, axis, route)


def rope_tables(segment, starts, heights, widths, counts):
    head_size = HD
    token_total = segment.shape[0]
    counter = jnp.arange(token_total, dtype=jnp.int32)
    slot_ids = jnp.arange(starts.shape[0], dtype=jnp.int32)
    first_index = jnp.sum((segment[None, :] < slot_ids[:, None]).astype(jnp.int32), axis=1)
    member = (segment[:, None] == slot_ids[None, :]).astype(jnp.int32)

    def choose(lookup_table):
        return jnp.sum(member * lookup_table[None, :], axis=1)

    begin_pos = choose(first_index)
    anchor = choose(starts)
    rows_tall = choose(heights)
    cols_broad = choose(widths)
    present = choose(counts)
    image_span = rows_tall * cols_broad * present
    offset = counter - anchor
    inside = (offset >= 0) & (offset < image_span)
    beyond = offset >= image_span
    relative = counter - begin_pos
    shifted = relative - image_span + present * jnp.maximum(rows_tall, cols_broad)
    text_pos = jnp.where(beyond, shifted, relative)
    base_pos = anchor - begin_pos
    clipped = jnp.maximum(offset, 0)
    grid_row = clipped // cols_broad
    grid_col = clipped % cols_broad
    temporal = jnp.where(inside, base_pos, text_pos).astype(jnp.float32)
    vertical = jnp.where(inside, base_pos + grid_row, text_pos).astype(jnp.float32)
    horizontal = jnp.where(inside, base_pos + grid_col, text_pos).astype(jnp.float32)
    freq_index = jnp.arange(head_size // 2, dtype=jnp.int32)
    inverse = jnp.exp(freq_index.astype(jnp.float32) * (-2.0 * math.log(rope_theta) / head_size))
    section = jnp.where(
        freq_index < head_size // 8,
        0,
        jnp.where(freq_index < head_size // 8 + 3 * head_size // 16, 1, 2),
    )
    angles = jnp.where(
        section[None, :] == 0,
        temporal[:, None] * inverse[None, :],
        jnp.where(
            section[None, :] == 1,
            vertical[:, None] * inverse[None, :],
            horizontal[:, None] * inverse[None, :],
        ),
    )
    doubled = jnp.concatenate([angles, angles], axis=-1)
    return (jnp.cos(doubled), jnp.sin(doubled))


def rotate(vectors, cosine, sine_table):
    half_size = vectors.shape[-1] // 2
    turned = jnp.concatenate([-vectors[..., half_size:], vectors[..., :half_size]], axis=-1)
    return vectors * cosine + turned * sine_table


def local(
    hidden_in,
    norm_gain,
    qkv_weight,
    qkv_bias,
    out_weight,
    segment_ids,
    image_start,
    image_height,
    image_width,
    image_count,
):
    micro_total = hidden_in.shape[0]
    phase = lax.axis_index("pipe")
    phases = lax.axis_size("pipe")
    tensor_size = lax.axis_size("tensor")
    query_width = out_weight.shape[1]
    query_heads = query_width // HD
    kv_heads = (qkv_weight.shape[2] - query_width) // (2 * HD)
    group_size = query_heads // kv_heads
    seq_tokens = segment_ids.shape[1]
    local_rows = seq_tokens // tensor_size
    model_width = hidden_in.shape[2] * tensor_size
    score_scale = 1.0 / math.sqrt(HD)
    gain_row = norm_gain[0][None, :]
    weight_local = qkv_weight[0]
    bias_local = qkv_bias[0][None, :]
    columns_local = out_weight[0]
    rows_all = lax.all_to_all(hidden_in, "tensor", split_axis=1, concat_axis=2, tiled=True)
    cosine_all, sine_all = jax.vmap(rope_tables)(
        segment_ids, image_start, image_height, image_width, image_count
    )
    counter = jnp.arange(seq_tokens, dtype=jnp.int32)
    allowed_all = (counter[None, :, None] >= counter[None, None, :]) & (
        segment_ids[:, :, None] == segment_ids[:, None, :]
    )

    def phase_step(step_index, loop_state):
        arriving, saved_rows = loop_state
        micro_index = step_index - phase
        active = (micro_index >= 0) & (micro_index < micro_total)
        chosen = jnp.clip(micro_index, 0, micro_total - 1)
        fresh_rows = lax.dynamic_index_in_dim(rows_all, chosen, 0, keepdims=False)
        residual = jnp.where(phase == 0, fresh_rows, arriving)
        widened = residual.astype(jnp.float32)
        scale_row = lax.rsqrt(jnp.mean(widened * widened, axis=-1, keepdims=True) + epsilon)
        normed = (widened * scale_row * gain_row).astype(jnp.bfloat16)
        gathered = lax.all_gather(normed, "tensor", axis=0, tiled=True)
        projected = jnp.dot(gathered, weight_local, preferred_element_type=jnp.float32) + bias_local
        cosine = lax.dynamic_index_in_dim(cosine_all, chosen, 0, keepdims=False)
        sine_table = lax.dynamic_index_in_dim(sine_all, chosen, 0, keepdims=False)
        allowed = lax.dynamic_index_in_dim(allowed_all, chosen, 0, keepdims=False)
        queries = projected[:, :query_width].reshape(seq_tokens, kv_heads, group_size, HD)
        queries = rotate(queries, cosine[:, None, None, :], sine_table[:, None, None, :]).astype(
            jnp.bfloat16
        )
        key_rows = projected[:, query_width : query_width + kv_heads * HD].reshape(
            seq_tokens, kv_heads, HD
        )
        key_rows = rotate(key_rows, cosine[:, None, :], sine_table[:, None, :]).astype(jnp.bfloat16)
        values = (
            projected[:, query_width + kv_heads * HD :]
            .reshape(seq_tokens, kv_heads, HD)
            .astype(jnp.bfloat16)
        )
        scores = (
            jnp.einsum("skgh,ukh->kgsu", queries, key_rows, preferred_element_type=jnp.float32)
            * score_scale
        )
        exponent = jnp.where(allowed[None, None, :, :], jnp.exp(scores), 0.0)
        weights = (exponent / jnp.sum(exponent, axis=-1, keepdims=True)).astype(jnp.bfloat16)
        attended = jnp.einsum("kgsu,ukh->skgh", weights, values, preferred_element_type=jnp.float32)
        attended = attended.astype(jnp.bfloat16).reshape(seq_tokens, query_width)
        partial_rows = jnp.dot(
            lax.all_gather(attended, "dp", axis=0, tiled=True),
            columns_local,
            preferred_element_type=jnp.float32,
        )
        streams = partial_rows.shape[0] // seq_tokens
        quartered = partial_rows.reshape(streams, tensor_size, local_rows, partial_rows.shape[1])
        summed = lax.psum_scatter(quartered, "tensor", scatter_dimension=1, tiled=True)
        returned = lax.all_to_all(summed, "dp", split_axis=0, concat_axis=3, tiled=True)
        update = returned.reshape(local_rows, model_width)
        result = (widened + update).astype(jnp.bfloat16)
        previous = lax.dynamic_index_in_dim(saved_rows, chosen, 0, keepdims=False)
        saved_rows = lax.dynamic_update_index_in_dim(
            saved_rows, jnp.where(active, result, previous), chosen, 0
        )
        arriving = shifted_2(result, "pipe", 1)
        return (arriving, saved_rows)

    initial_rows = jnp.zeros((local_rows, model_width), jnp.bfloat16)
    initial_saved = jnp.zeros((micro_total, local_rows, model_width), jnp.bfloat16)
    final_state = lax.fori_loop(
        0, phases + micro_total - 1, phase_step, (initial_rows, initial_saved)
    )
    layer_columns = lax.all_to_all(
        final_state[1], "tensor", split_axis=2, concat_axis=1, tiled=True
    )
    return layer_columns[None]


def solution(mesh):
    return jax.shard_map(
        local,
        mesh=mesh,
        in_specs=(
            P(None, "dp", "tensor"),
            P("pipe", None),
            P("pipe", None, "tensor"),
            P("pipe", "tensor"),
            P("pipe", "tensor", "dp"),
            P(None, "dp"),
            P(None, "dp"),
            P(None, "dp"),
            P(None, "dp"),
            P(None, "dp"),
        ),
        out_specs=P("pipe", None, "dp", "tensor"),
        check_vma=False,
    )
```

profile of v0, /device:TPU:7, one launch (start us, length us, event | category | flops | bytes accessed | tf_op | source)
XLA Modules:
  0.0 1156.9 jit_solution(12480396380980873604)
XLA Ops:
  9.4 3.6 copy.95
  13.6 7.1 reduce.7
  21.5 4.9 all_to_all.67
  29.7 1043.9 %while.17 = (s32[]{:T(128)}, bf16[64,8192]{1,0:T(8,128)(2,1)S(1)}, bf16[1,64,8192]{2,1,0:T(8,128)(2,1)}, pred[]{:T(512)}, bf16[1,64,8192]{2,1,0:T(8,128)(2,1)S(1...) while((s32[]{:T(128)}, bf16[64,8192]{1,0:T(8,128)(2,1)S(1)}, ...), condition=%wide.region_10.11_spmd.clone, body=%wide.region_6.10_spmd.clone.sunk | while | flops 9808545792 | bytes 221196528 | solution.py:170
  31.9 16.3 %all-gather.3.cloned.1.call-done = bf16[128,8192]{1,0:T(8,128)(2,1)} async-done(((bf16[64,8192]{1,0:T(8,128)(2,1)}), bf16[128,8192]{1,0:T(8,128)(2,1)}) %all-gather.3.cloned.1.call-update) | async-done | bytes 2097168 | tf_op jit(solution)/shard_map/while/body/eval_jaxpr/all_gather | solution.py:124
  48.2 16.4 %convolution_add_fusion.2 = f32[128,2560]{1,0:T(8,128)S(1)} fusion(bf16[128,8192]{1,0:T(8,128)(2,1)} %all-gather.3.cloned.1.call-done, bf16[8192,2560]{1,0:T(8,128)(2,1)} %get-tuple-element.472, f32[2560]{0:T(1024)S(1)} %reduce.10), kind=kOutput, calls=%fused_computation.1.clone.1 | convolution fusion | flops 5369036800 | bytes 45361152 | tf_op jit(solution)/shard_map/while/body/eval_jaxpr/dot_general | solution.py:125
  65.9 1.7 slice_negate_fusion.4
  69.9 3.4 fusion.66
  73.3 2.8 convolution_convert_fusion.2
  76.2 360.5 %all-gather.5.cloned.1.call-done = bf16[4096,2048]{0,1:T(8,128)(2,1)} async-done(((bf16[128,2048]{0,1:T(8,128)(2,1)}), bf16[4096,2048]{0,1:T(8,128)(2,1)}) %all-gather.5.cloned.1.call-update) | async-done | bytes 16777232 | tf_op jit(solution)/shard_map/while/body/eval_jaxpr/all_gather | solution.py:151
  436.7 10.2 fusion.67
  448.1 34.2 %all-reduce.5.cloned.1.call-done = f32[32,2,64,256]{3,2,1,0:T(8,128)} async-done(((f32[32,2,64,256]{3,2,1,0:T(8,128)}), f32[32,2,64,256]{3,2,1,0:T(8,128)}) %all-reduce.5.cloned.1.call-update) | async-done | bytes 4194320 | tf_op jit(solution)/shard_map/while
  482.3 3.7 constant_dynamic-slice_fusion.2
  486.0 7.9 all-to-all-start
  494.0 28.2 %all-to-all-done = f32[32,1,64,256]{3,2,1,0:T(8,128)S(1)} async-done(((f32[32,1,64,256]{3,2,1,0:T(8,128)}), f32[32,1,64,256]{3,2,1,0:T(8,128)S(1)}, u32[]{:S(2)}, u32[]{:S(2)}) %all-to-all-start) | async-done | bytes 2097184 | tf_op jit(solution)/shard_map/while/body/eval_jaxpr/all_to_all | solution.py:158
  527.2 25.2 %collective-permute-done = bf16[64,8192]{1,0:T(8,128)(2,1)S(1)} collective-permute-done((bf16[64,8192]{1,0:T(8,128)(2,1)}, bf16[64,8192]{1,0:T(8,128)(2,1)S(1)}, u32[]{:S(2)}, u32[]{:S(2)}) %collective-permute-start) | collective-permute-done | bytes 1048608 | tf_op jit(solution)/shard_map/while/body/eval_jaxpr/ppermute | solution.py:18
  554.4 14.9 %all-gather.3.cloned.1.call-done = bf16[128,8192]{1,0:T(8,128)(2,1)} async-done(((bf16[64,8192]{1,0:T(8,128)(2,1)}), bf16[128,8192]{1,0:T(8,128)(2,1)}) %all-gather.3.cloned.1.call-update) | async-done | bytes 2097168 | tf_op jit(solution)/shard_map/while/body/eval_jaxpr/all_gather | solution.py:124
  569.4 16.4 %convolution_add_fusion.2 = f32[128,2560]{1,0:T(8,128)S(1)} fusion(bf16[128,8192]{1,0:T(8,128)(2,1)} %all-gather.3.cloned.1.call-done, bf16[8192,2560]{1,0:T(8,128)(2,1)} %get-tuple-element.472, f32[2560]{0:T(1024)S(1)} %reduce.10), kind=kOutput, calls=%fused_computation.1.clone.1 | convolution fusion | flops 5369036800 | bytes 45361152 | tf_op jit(solution)/shard_map/while/body/eval_jaxpr/dot_general | solution.py:125
  591.0 3.4 fusion.66
  594.5 2.8 convolution_convert_fusion.2
  597.3 360.5 %all-gather.5.cloned.1.call-done = bf16[4096,2048]{0,1:T(8,128)(2,1)} async-done(((bf16[128,2048]{0,1:T(8,128)(2,1)}), bf16[4096,2048]{0,1:T(8,128)(2,1)}) %all-gather.5.cloned.1.call-update) | async-done | bytes 16777232 | tf_op jit(solution)/shard_map/while/body/eval_jaxpr/all_gather | solution.py:151
  957.8 10.2 fusion.67
  969.3 34.2 %all-reduce.5.cloned.1.call-done = f32[32,2,64,256]{3,2,1,0:T(8,128)} async-done(((f32[32,2,64,256]{3,2,1,0:T(8,128)}), f32[32,2,64,256]{3,2,1,0:T(8,128)}) %all-reduce.5.cloned.1.call-update) | async-done | bytes 4194320 | tf_op jit(solution)/shard_map/while
  1003.5 3.7 constant_dynamic-slice_fusion.2
  1007.2 7.9 all-to-all-start
  1015.1 28.2 %all-to-all-done = f32[32,1,64,256]{3,2,1,0:T(8,128)S(1)} async-done(((f32[32,1,64,256]{3,2,1,0:T(8,128)}), f32[32,1,64,256]{3,2,1,0:T(8,128)S(1)}, u32[]{:S(2)}, u32[]{:S(2)}) %all-to-all-start) | async-done | bytes 2097184 | tf_op jit(solution)/shard_map/while/body/eval_jaxpr/all_to_all | solution.py:158
  1048.3 25.2 %collective-permute-done = bf16[64,8192]{1,0:T(8,128)(2,1)S(1)} collective-permute-done((bf16[64,8192]{1,0:T(8,128)(2,1)}, bf16[64,8192]{1,0:T(8,128)(2,1)S(1)}, u32[]{:S(2)}, u32[]{:S(2)}) %collective-permute-start) | collective-permute-done | bytes 1048608 | tf_op jit(solution)/shard_map/while/body/eval_jaxpr/ppermute | solution.py:18
  1073.5 9.2 copy.71
  1082.7 45.5 %reduce.8 = bf16[8192,64]{1,0:T(8,128)(2,1)S(1)} reduce(bf16[8192,1,64]{2,1,0:T(2,128)(2,1)} %bitcast.148, bf16[]{:T(256)} %broadcast.908), dimensions={1}, to_apply=%bitcast.75.reduce_sub_computation | reduce | bytes 2097154
  1129.8 6.9 all_to_all.68
  1136.7 2.7 reshape.1275
  1139.5 8.2 copy.72
  (105 shorter events, 36.8 us)
Async XLA Ops:
  28.4 1.3 copy-start.4
  28.4 1.3 copy-start.6
  28.4 1.2 copy-start.8
  29.9 1.9 copy-start.2
  29.9 18.4 %all-gather.3.cloned.1.call-start = ((), (), s32[]{:S(2)}) async-start(), calls=%async_computation.3 | async-start | bytes 3145728 | tf_op jit(solution)/shard_map/while/body/eval_jaxpr/all_gather | solution.py:124
  31.7 404.9 %all-gather.5.cloned.1.call-start = ((), (), s32[]{:S(2)}) async-start(), calls=%async_computation.4 | async-start | bytes 17301504 | tf_op jit(solution)/shard_map/while/body/eval_jaxpr/all_gather | solution.py:151
  73.3 363.4 %copy-start.10 = (bf16[2048,256]{1,0:T(8,128)(2,1)S(1)}, bf16[2048,256]{1,0:T(8,128)(2,1)}, u32[]{:S(2)}) copy-start(bf16[2048,256]{1,0:T(8,128)(2,1)} %get-tuple-element.476) | copy-start | bytes 3145732 | tf_op jit(solution)/shard_map/while
  76.1 406.2 %all-reduce.5.cloned.1.call-start = ((), (), s32[]{:S(2)}) async-start(), calls=%async_computation.5 | async-start | bytes 8388608 | tf_op jit(solution)/shard_map/while
  446.9 0.7 copy-start.11
  486.0 36.1 %all-to-all-start = ((f32[32,1,64,256]{3,2,1,0:T(8,128)}), f32[32,1,64,256]{3,2,1,0:T(8,128)S(1)}, u32[]{:S(2)}, u32[]{:S(2)}) async-start(f32[32,1,64,256]{3,2,1,0:T(8,128)} %constant_dynamic-slice_fusion.2), calls=%async_computation | async-start | bytes 4194304 | tf_op jit(solution)/shard_map/while/body/eval_jaxpr/all_to_all | solution.py:158
  522.1 1.2 copy-start
  523.3 29.0 %copy-start.3 = (bf16[1,64,8192]{2,1,0:T(8,128)(2,1)S(1)}, bf16[1,64,8192]{2,1,0:T(8,128)(2,1)}, u32[]{:S(2)}) copy-start(bf16[1,64,8192]{2,1,0:T(8,128)(2,1)} %copy-done.2) | copy-start | bytes 3145732 | tf_op jit(solution)/shard_map/while
  523.3 29.0 %copy-start.5 = (f32[1,8192]{1,0:T(1,128)S(1)}, f32[1,8192]{1,0:T(1,128)}, u32[]{:S(2)}) copy-start(f32[1,8192]{1,0:T(1,128)} %get-tuple-element.517) | copy-start | bytes 98308 | tf_op jit(solution)/shard_map/while
  523.4 29.0 %copy-start.7 = (f32[1,2560]{1,0:T(1,128)S(1)}, f32[1,2560]{1,0:T(1,128)}, u32[]{:S(2)}) copy-start(f32[1,2560]{1,0:T(1,128)} %get-tuple-element.537) | copy-start | bytes 30724 | tf_op jit(solution)/shard_map/while
  523.4 29.0 %copy-start.9 = (s32[1,128]{1,0:T(1,128)S(1)}, s32[1,128]{1,0:T(1,128)}, u32[]{:S(2)}) copy-start(s32[1,128]{1,0:T(1,128)} %get-tuple-element.558) | copy-start | bytes 1540 | tf_op jit(solution)/shard_map/while
  524.9 1.0 copy-start.1
  525.9 26.5 %collective-permute-start = (bf16[64,8192]{1,0:T(8,128)(2,1)}, bf16[64,8192]{1,0:T(8,128)(2,1)S(1)}, u32[]{:S(2)}, u32[]{:S(2)}) collective-permute-start(bf16[64,8192]{1,0:T(8,128)(2,1)} %get-tuple-element.428), channel_id=1, source_target_pairs={{0,64},{1,65},{2,66},{3,67},{4,68},{5,69},{6,70},{7,71},{8,72},{9,... | collective-permute-start | bytes 3145736 | tf_op jit(solution)/shard_map/while/body/eval_jaxpr/ppermute | solution.py:18
  552.4 1.9 copy-start.2
  552.4 17.0 %all-gather.3.cloned.1.call-start = ((), (), s32[]{:S(2)}) async-start(), calls=%async_computation.3 | async-start | bytes 3145728 | tf_op jit(solution)/shard_map/while/body/eval_jaxpr/all_gather | solution.py:124
  554.3 403.6 %all-gather.5.cloned.1.call-start = ((), (), s32[]{:S(2)}) async-start(), calls=%async_computation.4 | async-start | bytes 17301504 | tf_op jit(solution)/shard_map/while/body/eval_jaxpr/all_gather | solution.py:151
  594.5 363.4 %copy-start.10 = (bf16[2048,256]{1,0:T(8,128)(2,1)S(1)}, bf16[2048,256]{1,0:T(8,128)(2,1)}, u32[]{:S(2)}) copy-start(bf16[2048,256]{1,0:T(8,128)(2,1)} %get-tuple-element.476) | copy-start | bytes 3145732 | tf_op jit(solution)/shard_map/while
  597.3 406.2 %all-reduce.5.cloned.1.call-start = ((), (), s32[]{:S(2)}) async-start(), calls=%async_computation.5 | async-start | bytes 8388608 | tf_op jit(solution)/shard_map/while
  968.0 0.7 copy-start.11
  1007.2 36.1 %all-to-all-start = ((f32[32,1,64,256]{3,2,1,0:T(8,128)}), f32[32,1,64,256]{3,2,1,0:T(8,128)S(1)}, u32[]{:S(2)}, u32[]{:S(2)}) async-start(f32[32,1,64,256]{3,2,1,0:T(8,128)} %constant_dynamic-slice_fusion.2), calls=%async_computation | async-start | bytes 4194304 | tf_op jit(solution)/shard_map/while/body/eval_jaxpr/all_to_all | solution.py:158
  1043.3 1.2 copy-start
  1044.5 29.0 %copy-start.3 = (bf16[1,64,8192]{2,1,0:T(8,128)(2,1)S(1)}, bf16[1,64,8192]{2,1,0:T(8,128)(2,1)}, u32[]{:S(2)}) copy-start(bf16[1,64,8192]{2,1,0:T(8,128)(2,1)} %copy-done.2) | copy-start | bytes 3145732 | tf_op jit(solution)/shard_map/while
  1044.5 29.0 %copy-start.5 = (f32[1,8192]{1,0:T(1,128)S(1)}, f32[1,8192]{1,0:T(1,128)}, u32[]{:S(2)}) copy-start(f32[1,8192]{1,0:T(1,128)} %get-tuple-element.517) | copy-start | bytes 98308 | tf_op jit(solution)/shard_map/while
  1044.5 29.0 %copy-start.7 = (f32[1,2560]{1,0:T(1,128)S(1)}, f32[1,2560]{1,0:T(1,128)}, u32[]{:S(2)}) copy-start(f32[1,2560]{1,0:T(1,128)} %get-tuple-element.537) | copy-start | bytes 30724 | tf_op jit(solution)/shard_map/while
  1044.5 29.0 %copy-start.9 = (s32[1,128]{1,0:T(1,128)S(1)}, s32[1,128]{1,0:T(1,128)}, u32[]{:S(2)}) copy-start(s32[1,128]{1,0:T(1,128)} %get-tuple-element.558) | copy-start | bytes 1540 | tf_op jit(solution)/shard_map/while
  1046.1 1.0 copy-start.1
  1047.1 26.5 %collective-permute-start = (bf16[64,8192]{1,0:T(8,128)(2,1)}, bf16[64,8192]{1,0:T(8,128)(2,1)S(1)}, u32[]{:S(2)}, u32[]{:S(2)}) collective-permute-start(bf16[64,8192]{1,0:T(8,128)(2,1)} %get-tuple-element.428), channel_id=1, source_target_pairs={{0,64},{1,65},{2,66},{3,67},{4,68},{5,69},{6,70},{7,71},{8,72},{9,... | collective-permute-start | bytes 3145736 | tf_op jit(solution)/shard_map/while/body/eval_jaxpr/ppermute | solution.py:18
Sparse Core Ops, SparseCore 0:
  32.4 15.8 all-gather.2
  76.2 360.3 all-gather.4
  447.0 35.2 all-reduce.4
  554.6 14.7 all-gather.2
  597.4 360.3 all-gather.4
  968.2 35.2 all-reduce.4
where the time goes:
time: 1160 us
  waiting for transfers between devices  927 us (80%)
  other arithmetic  67.1 us (6%)
  matrix products  65.7 us (6%)
  local copies, waits for them, and re-layouts  52.2 us (4%)
  starting transfers between devices  18.7 us (2%)
  between operations  13.5 us (1%)
  blocking collectives  11.8 us (1%)
    all_gather x2, waiting for transfers between devices, phase_step(): lax.all_gather(attended, 'dp', axis=0, tiled=True)  721 us
    while x8, waiting for transfers between devices  68.4 us
    all_to_all x2, waiting for transfers between devices, phase_step(): lax.all_to_all(summed, 'dp', split_axis=0, concat_axis=3, tiled=True)  56.3 us
    unnamed x2, other arithmetic  52.5 us
    ppermute x2, waiting for transfers between devices, shifted_2(): return lax.ppermute(block, axis, route)  50.3 us
    dot_general x2, matrix products, phase_step(): jnp.dot(gathered, weight_local, preferred_element_type=jnp.float32)  32.9 us
    all_gather x2, waiting for transfers between devices, phase_step(): gathered = lax.all_gather(normed, 'tensor', axis=0, tiled=True)  31.3 us
  transfers between devices with their start and end apart: 10, of which 10 were waited for; matrix products, arithmetic and copies ran while one was open for 0% of the time, Pallas kernels for 0%

commit v1 on v0

v1 whole, which is shorter than its diff:
```python
import math

import jax
import jax.numpy as jnp
from jax import lax
from jax.experimental import pallas as pl
from jax.experimental.pallas import tpu as pltpu
from jax.sharding import PartitionSpec as P

HD = 128
SEQ = 128
D = 8192
HALF = 4096
QUERY = 2048
CHUNK = 256
CHUNKS = 10
SLOTS = 8
PIECES = 4
PIECE = 512
GROUP = 8
BLOCK = 256
THETA = 1000000.0
EPSILON = 1e-06
MIB = 1 << 20
MESH = pl.DeviceIdType.MESH


def copy_to(src, dst, send, recv, device):
    return pltpu.make_async_remote_copy(
        src_ref=src,
        dst_ref=dst,
        send_sem=send,
        recv_sem=recv,
        device_id=device,
        device_id_type=MESH,
    )


def rotary_tables(seg_ref, start_ref, height_ref, width_ref, count_ref):
    row = lax.broadcasted_iota(jnp.int32, (SEQ, SEQ), 0)
    lane = lax.broadcasted_iota(jnp.int32, (SEQ, SEQ), 1)
    seg_keys = jnp.broadcast_to(seg_ref[...].astype(jnp.float32), (SEQ, SEQ))
    seg = jnp.sum(jnp.where(row == lane, seg_keys, 0.0), axis=1, keepdims=True)
    seg = jnp.broadcast_to(seg, (SEQ, SEQ))
    allowed = (row >= lane) & (seg == seg_keys)
    border = jnp.sum(jnp.where(seg_keys == 0.0, 1.0, 0.0), axis=1, keepdims=True)
    first = seg == 0.0

    def choose(ref):
        return jnp.where(
            first, ref[0, 0].astype(jnp.float32), ref[0, 1].astype(jnp.float32)
        )

    begin = jnp.where(first, 0.0, border)
    anchor = choose(start_ref)
    tall = choose(height_ref)
    broad = choose(width_ref)
    present = choose(count_ref)
    counter = row.astype(jnp.float32)
    span = tall * broad * present
    offset = counter - anchor
    inside = (offset >= 0.0) & (offset < span)
    relative = counter - begin
    shifted = relative - span + present * jnp.maximum(tall, broad)
    text = jnp.where(offset >= span, shifted, relative)
    base = anchor - begin
    clipped = jnp.maximum(offset, 0.0)
    grid_row = jnp.floor((clipped + 0.5) / broad)
    grid_col = clipped - grid_row * broad
    freq = lane % (HD // 2)
    inverse = jnp.exp(freq.astype(jnp.float32) * (-2.0 * math.log(THETA) / HD))
    moved = jnp.where(
        freq < HD // 8, 0.0, jnp.where(freq < HD // 8 + 3 * HD // 16, grid_row, grid_col)
    )
    angles = jnp.where(inside, base + moved, text) * inverse
    sine = jnp.sin(angles)
    return jnp.cos(angles), jnp.where(lane < HD // 2, -sine, sine), allowed


def kernel(
    hidden,
    gain,
    qkv,
    bias,
    out_weight,
    seg,
    start,
    height,
    width,
    count,
    out,
    wbuf,
    gathered,
    weights,
    scaled,
    squares,
    x_own,
    x_in,
    x_relay,
    total,
    part_out,
    part_in,
    sums,
    landed,
    cosine,
    sine,
    mask,
    rows,
    keys,
    values,
    w_sem,
    local_sem,
    ws,
    wr,
    a_s,
    a_r,
    x_s,
    x_r,
    p_s,
    p_r,
    c_s,
    c_r,
    r_s,
    r_r,
    f_s,
    f_r,
):
    p = lax.axis_index("pipe")
    d = lax.axis_index("dp")
    t = lax.axis_index("tensor")
    xl = d % 2
    y = (d // 2) % 4
    z = d // 8

    def at(y_, xl_):
        return (y_ % 4) * 2 + xl_

    def device(slot, pipe=p, z_=z):
        return (pipe, (z_ % 4) * 8 + slot, t)

    own = at(y, xl)
    other_core = (p, d, 1 - t)
    partner = device(at(y, 1 - xl))
    y_up, y_down = device(at(y + 1, xl)), device(at(y + 3, xl))
    z_up, z_down = device(own, z_=z + 1), device(own, z_=z + 3)
    across = device(at(y, 1 - xl), pipe=1 - p)

    def weight_copy(step):
        chunk = (step + 8) % CHUNKS
        slot = step % SLOTS
        return pltpu.make_async_copy(
            qkv.at[:, pl.ds(pl.multiple_of(chunk * CHUNK, CHUNK), CHUNK)],
            wbuf.at[slot],
            w_sem.at[slot],
        )

    for step in range(SLOTS):
        weight_copy(step).start()
    own_weights = [
        pltpu.make_async_copy(
            out_weight.at[pl.ds(k * PIECE, PIECE)], weights.at[z, k], local_sem.at[k]
        )
        for k in range(PIECES)
    ]
    for copy in own_weights:
        copy.start()

    barrier = pltpu.get_barrier_semaphore()
    pl.semaphore_signal(barrier, inc=1, device_id=other_core, device_id_type=MESH)
    for to in (z_up, z_down):
        pl.semaphore_signal(barrier, inc=1, device_id=to, device_id_type=MESH)
    for j in range(GROUP):
        slot = (own + j) % GROUP
        pl.semaphore_signal(
            barrier, inc=1, device_id=device(slot, pipe=1 - p), device_id_type=MESH
        )
        if j:
            pl.semaphore_signal(barrier, inc=1, device_id=device(slot), device_id_type=MESH)
    pl.semaphore_wait(barrier, 2 * GROUP + 2)

    def weight_up(k):
        src = out_weight.at[pl.ds(k * PIECE, PIECE)]
        return copy_to(src, weights.at[z, k], ws.at[0, k], wr.at[0, k], z_up)

    def weight_down(k):
        src = out_weight.at[pl.ds(k * PIECE, PIECE)]
        return copy_to(src, weights.at[z, k], ws.at[1, k], wr.at[1, k], z_down)

    def weight_pass_up(k):
        ref = weights.at[(z + 3) % 4, k, pl.ds(0, PIECE // 2)]
        return copy_to(ref, ref, ws.at[2, k], wr.at[2, k], z_up)

    def weight_pass_down(k):
        ref = weights.at[(z + 1) % 4, k, pl.ds(PIECE // 2, PIECE // 2)]
        return copy_to(ref, ref, ws.at[3, k], wr.at[3, k], z_down)

    for k in range(PIECES):
        weight_up(k).start()
        weight_down(k).start()

    half = SEQ // 2

    def rows_copy(k, kind):
        ref, to = {
            0: (gathered.at[k, own], partner),
            1: (gathered.at[k, own], y_up),
            2: (gathered.at[k, own], y_down),
            3: (gathered.at[k, at(y, 1 - xl)], y_up),
            4: (gathered.at[k, at(y, 1 - xl)], y_down),
            5: (gathered.at[k, at(y + 3, xl), pl.ds(0, half)], y_up),
            6: (gathered.at[k, at(y + 1, xl), pl.ds(half, half)], y_down),
            7: (gathered.at[k, at(y + 2, xl)], partner),
        }[kind]
        return copy_to(ref, ref, a_s.at[kind, k], a_r.at[kind, k], to)

    def inject(k):
        for kind in (1, 2, 0):
            rows_copy(k, kind).start()

    def pass_first(k):
        rows_copy(k, 0).wait_recv()
        rows_copy(k, 3).start()
        rows_copy(k, 4).start()
        rows_copy(k, 1).wait_recv()
        rows_copy(k, 5).start()
        rows_copy(k, 2).wait_recv()
        rows_copy(k, 6).start()

    def pass_second(k):
        rows_copy(k, 5).wait_recv()
        rows_copy(k, 6).wait_recv()
        rows_copy(k, 7).start()

    def pass_weights(k):
        weight_up(k).wait_recv()
        weight_pass_up(k).start()
        weight_down(k).wait_recv()
        weight_pass_down(k).start()

    send_hidden = copy_to(hidden, x_relay, r_s, r_r, across)
    send_x = copy_to(x_own, x_relay, r_s, r_r, across)
    pass_hidden = copy_to(x_relay, x_in, f_s, f_r, partner)
    pass_x = copy_to(x_relay, out, f_s, f_r, partner)
    load_hidden = pltpu.make_async_copy(hidden, x_own, local_sem.at[PIECES])

    @pl.when(p == 0)
    def _():
        load_hidden.start()
        send_hidden.start()

    cos, sin, allowed = rotary_tables(seg, start, height, width, count)
    cosine[...] = cos
    sine[...] = sin
    mask[...] = jnp.where(allowed, 1.0, 0.0)

    def sums_copy(slot):
        return copy_to(
            sums.at[slot], landed.at[p, own], c_s.at[slot], c_r.at[p, own], device(slot, pipe=1)
        )

    def landed_wait(layer, slot):
        pltpu.make_async_copy(
            landed.at[layer, slot], landed.at[layer, slot], c_r.at[layer, slot]
        ).wait()

    def add_update(layer, source):
        def body(slot, carry):
            for zz in range(2):
                cols = pl.ds(pl.multiple_of(zz * 2048 + slot * BLOCK, BLOCK), BLOCK)
                x_own[:, cols] = (
                    source[:, cols].astype(jnp.float32)
                    + landed[layer, slot, zz].astype(jnp.float32)
                ).astype(jnp.bfloat16)
            return carry

        lax.fori_loop(0, GROUP, body, 0)

    @pl.when(p == 0)
    def _():
        load_hidden.wait()

    @pl.when(p == 1)
    def _():
        send_hidden.wait_recv()
        pass_hidden.start()
        pass_hidden.wait_recv()
        for slot in range(GROUP):
            landed_wait(0, slot)
        add_update(0, x_in)
        send_x.start()

    def scale_body(j, square):
        cols = pl.ds(pl.multiple_of(j * 512, 512), 512)
        x = x_own[:, cols].astype(jnp.float32)
        g = gain[:, pl.ds(pl.multiple_of(t * HALF + j * 512, 512), 512)]
        scaled[t, :, cols] = (x * g).astype(jnp.bfloat16)
        x = x * x
        return square + x[:, 0:128] + x[:, 128:256] + x[:, 256:384] + x[:, 384:512]

    square = lax.fori_loop(0, HALF // 512, scale_body, jnp.zeros((SEQ, 128), jnp.float32))
    squares[t] = square
    scaled_copy = copy_to(scaled.at[t], scaled.at[t], x_s.at[0], x_r.at[0], other_core)
    squares_copy = copy_to(squares.at[t], squares.at[t], x_s.at[1], x_r.at[1], other_core)
    scaled_copy.start()
    squares_copy.start()
    squares_copy.wait_recv()
    scaled_copy.wait_recv()
    mean = jnp.sum(squares[0] + squares[1], axis=1, keepdims=True) * (1.0 / D)
    rows[...] = jnp.broadcast_to(lax.rsqrt(mean + EPSILON), (SEQ, SEQ))

    def rotated(u):
        return (u * cosine[...] + pltpu.roll(u, HD // 2, 1) * sine[...]).astype(jnp.bfloat16)

    def project(step, carry):
        slot = step % SLOTS
        chunk = (step + 8) % CHUNKS
        weight_copy(step).wait()
        u = jnp.dot(scaled[0], wbuf[slot, 0:HALF], preferred_element_type=jnp.float32)
        u += jnp.dot(scaled[1], wbuf[slot, HALF:D], preferred_element_type=jnp.float32)
        scale = rows[...]
        b = bias[:, pl.ds(pl.multiple_of(chunk * CHUNK, CHUNK), CHUNK)]
        heads = [u[:, h * HD : (h + 1) * HD] * scale + b[:, h * HD : (h + 1) * HD] for h in range(2)]

        @pl.when(step + SLOTS < CHUNKS)
        def _():
            weight_copy(step + SLOTS).start()

        @pl.when(step == 0)
        def _():
            for h in range(2):
                keys[h] = rotated(heads[h])

        @pl.when(step == 1)
        def _():
            for h in range(2):
                values[h] = heads[h].astype(jnp.bfloat16)

        @pl.when(step >= 2)
        def _():
            q_chunk = step - 2
            kv = q_chunk // 4
            for h in range(2):
                scores = lax.dot_general(
                    rotated(heads[h]),
                    keys[kv],
                    (((1,), (1,)), ((), ())),
                    preferred_element_type=jnp.float32,
                ) * (1.0 / math.sqrt(HD))
                exponent = jnp.where(mask[...] > 0.0, jnp.exp(scores), 0.0)
                weight = exponent / jnp.sum(exponent, axis=1, keepdims=True)
                attended = jnp.dot(
                    weight.astype(jnp.bfloat16), values[kv], preferred_element_type=jnp.float32
                )
                cols = pl.multiple_of((q_chunk % 2) * CHUNK + h * HD, HD)
                gathered[q_chunk // 2, own, :, pl.ds(cols, HD)] = attended.astype(jnp.bfloat16)

            @pl.when(q_chunk % 2 == 1)
            def _():
                inject(q_chunk // 2)

            @pl.when((q_chunk % 2 == 1) & (q_chunk >= 5))
            def _():
                pass_first(q_chunk // 2 - 2)

        return carry

    lax.fori_loop(0, CHUNKS, project, 0)

    def multiply(k):
        for kind in (3, 4, 7):
            rows_copy(k, kind).wait_recv()
        weight_pass_up(k).wait_recv()
        weight_pass_down(k).wait_recv()
        own_weights[k].wait()

        def body(j, carry):
            zb = (2 * (1 - t) + j // 2) % 4
            streams = pl.ds(pl.multiple_of((j % 2) * 4, 4), 4)
            part = jnp.dot(
                gathered[k, streams].reshape(4 * SEQ, PIECE),
                weights[zb, k],
                preferred_element_type=jnp.float32,
            ).reshape(4, SEQ, BLOCK)
            if k:
                part += total[zb, streams]
            if k < PIECES - 1:
                total[zb, streams] = part
            else:

                @pl.when(j < 4)
                def _():
                    part_out[j // 2, streams] = part.astype(jnp.bfloat16)

                @pl.when(j >= 4)
                def _():
                    total[zb, streams] = part

                @pl.when((j == 1) | (j == 3))
                def _():
                    part_copy(j // 2).start()

            return carry

        lax.fori_loop(0, 8, body, 0)

    def part_copy(zz):
        return copy_to(part_out.at[zz], part_in.at[zz], p_s.at[zz], p_r.at[zz], other_core)

    pass_weights(0)
    pass_weights(1)
    pass_first(2)
    pass_first(3)
    pass_weights(2)
    pass_second(0)
    pass_weights(3)
    pass_second(1)
    pass_second(2)
    multiply(0)
    pass_second(3)
    multiply(1)
    multiply(2)
    multiply(3)

    for zz in range(2):
        part_copy(zz).wait_recv()

    def finish(j, carry):
        slot = (own + 1 + j) % GROUP
        for zz in range(2):
            sums[slot, zz] = (
                total[2 * t + zz, slot] + part_in[zz, slot].astype(jnp.float32)
            ).astype(jnp.bfloat16)

        @pl.when((p == 0) | (j < GROUP - 1))
        def _():
            sums_copy(slot).start()

        return carry

    lax.fori_loop(0, GROUP, finish, 0)

    @pl.when(p == 0)
    def _():
        send_x.wait_recv()
        pass_x.start()
        for slot in range(GROUP):
            sums_copy(slot).wait_send()
        send_hidden.wait_send()
        pass_x.wait()

    @pl.when(p == 1)
    def _():
        for zz in range(2):
            landed[1, own, zz] = sums[own, zz]
        for j in range(1, GROUP):
            landed_wait(1, (own + j) % GROUP)
        send_x.wait_send()
        add_update(1, x_own)
        store = pltpu.make_async_copy(x_own, out, local_sem.at[PIECES])
        store.start()
        for j in range(1, GROUP):
            sums_copy((own + j) % GROUP).wait_send()
        pass_hidden.wait_send()
        store.wait()

    for k in range(PIECES):
        for copy in (weight_up(k), weight_down(k), weight_pass_up(k), weight_pass_down(k)):
            copy.wait_send()
        for kind in range(8):
            rows_copy(k, kind).wait_send()
    scaled_copy.wait_send()
    squares_copy.wait_send()
    for zz in range(2):
        part_copy(zz).wait_send()


def local(hidden, gain, qkv, bias, out_weight, segment, start, height, width, count):
    bf16, f32 = jnp.bfloat16, jnp.float32
    anywhere = pl.BlockSpec(memory_space=pl.ANY)
    vmem = pl.BlockSpec(memory_space=pltpu.VMEM)
    smem = pl.BlockSpec(memory_space=pltpu.SMEM)
    dma = pltpu.SemaphoreType.DMA
    result = pl.pallas_call(
        kernel,
        out_shape=jax.ShapeDtypeStruct((SEQ, HALF), bf16),
        in_specs=[anywhere, vmem, anywhere, vmem, anywhere, vmem, smem, smem, smem, smem],
        out_specs=anywhere,
        scratch_shapes=[
            pltpu.VMEM((SLOTS, D, CHUNK), bf16),
            pltpu.VMEM((PIECES, GROUP, SEQ, PIECE), bf16),
            pltpu.VMEM((4, PIECES, PIECE, BLOCK), bf16),
            pltpu.VMEM((2, SEQ, HALF), bf16),
            pltpu.VMEM((2, SEQ, 128), f32),
            pltpu.VMEM((SEQ, HALF), bf16),
            pltpu.VMEM((SEQ, HALF), bf16),
            pltpu.VMEM((SEQ, HALF), bf16),
            pltpu.VMEM((4, GROUP, SEQ, BLOCK), f32),
            pltpu.VMEM((2, GROUP, SEQ, BLOCK), bf16),
            pltpu.VMEM((2, GROUP, SEQ, BLOCK), bf16),
            pltpu.VMEM((GROUP, 2, SEQ, BLOCK), bf16),
            pltpu.VMEM((2, GROUP, 2, SEQ, BLOCK), bf16),
            pltpu.VMEM((SEQ, SEQ), f32),
            pltpu.VMEM((SEQ, SEQ), f32),
            pltpu.VMEM((SEQ, SEQ), f32),
            pltpu.VMEM((SEQ, SEQ), f32),
            pltpu.VMEM((2, SEQ, HD), bf16),
            pltpu.VMEM((2, SEQ, HD), bf16),
            dma((SLOTS,)),
            dma((PIECES + 1,)),
            dma((4, PIECES)),
            dma((4, PIECES)),
            dma((8, PIECES)),
            dma((8, PIECES)),
            dma((2,)),
            dma((2,)),
            dma((2,)),
            dma((2,)),
            dma((GROUP,)),
            dma((2, GROUP)),
            dma(()),
            dma(()),
            dma(()),
            dma(()),
        ],
        compiler_params=pltpu.CompilerParams(
            collective_id=0, has_side_effects=True, vmem_limit_bytes=61 * MIB
        ),
        name="sublayers",
    )(
        hidden[0],
        gain,
        qkv[0],
        bias,
        out_weight[0],
        segment,
        start,
        height,
        width,
        count,
    )
    return result[None, None]


def solution(mesh):
    return jax.shard_map(
        local,
        mesh=mesh,
        in_specs=(
            P(None, "dp", "tensor"),
            P("pipe", None),
            P("pipe", None, "tensor"),
            P("pipe", "tensor"),
            P("pipe", "tensor", "dp"),
            P(None, "dp"),
            P(None, "dp"),
            P(None, "dp"),
            P(None, "dp"),
            P(None, "dp"),
        ),
        out_specs=P("pipe", None, "dp", "tensor"),
        check_vma=False,
    )
```

time: 1160 us -> 151 us (0.13)
  waiting for transfers between devices: 927 us -> 0 us
  Pallas kernels: 0 us -> 149 us
  other arithmetic: 67.1 us -> 0 us
  matrix products: 65.7 us -> 0 us
  local copies, waits for them, and re-layouts: 52.2 us -> 2.29 us
  starting transfers between devices: 18.7 us -> 0 us
  between operations: 13.5 us -> 0.01 us
  blocking collectives: 11.8 us -> 0 us
    all_gather x4 -> x0, waiting for transfers between devices: 752 us -> none  [the longest x2 721 us: phase_step(): lax.all_gather(attended, 'dp', axis=0, tiled=True)]
    pallas_call x0 -> x1, Pallas kernels: none -> 149 us  [local(): pl.pallas_call(kernel, out_shape=jax.ShapeDtypeStruct((SEQ, HALF), bf16),...]
    while x8 -> x0, waiting for transfers between devices: 68.4 us -> none
    dot_general x8 -> x0, matrix products: 65.7 us -> none  [the longest x2 32.9 us: phase_step(): jnp.dot(gathered, weight_local, preferred_element_type=jnp.float32)]
    all_to_all x2 -> x0, waiting for transfers between devices: 56.3 us -> none  [phase_step(): lax.all_to_all(summed, 'dp', split_axis=0, concat_axis=3, tiled=True)]
    unnamed x2 -> x0, other arithmetic: 52.5 us -> none
    ppermute x2 -> x0, waiting for transfers between devices: 50.3 us -> none  [shifted_2(): return lax.ppermute(block, axis, route)]
    while x47 -> x0, local copies, waits for them, and re-layouts: 24 us -> none
  transfers between devices with their start and end apart: 10 -> 0, of which waited for: 10 -> 0; matrix products, arithmetic and copies ran while one was open for 0% -> 0% of each run, Pallas kernels for 0% -> 0%
where the time goes in v1:
time: 151 us
  Pallas kernels  149 us (99%)
  local copies, waits for them, and re-layouts  2.29 us (2%)
    pallas_call x1, Pallas kernels, local(): pl.pallas_call(kernel, out_shape=jax.ShapeDtypeStruct((SEQ, HALF), bf16),...  149 us

profile of v1, /device:TPU:7, one launch (start us, length us, event | category | flops | bytes accessed | tf_op | source)
XLA Modules:
  0.0 151.2 jit_solution(3392943163659200740)
XLA Ops:
  0.0 148.9 %sublayers.1 = bf16[128,4096]{1,0:T(8,128)(2,1)} custom-call(bf16[128,4096]{1,0:T(8,128)(2,1)} %bitcast.6, f32[1,8192]{1,0:T(1,128)} %gain.1, bf16[8192,2560]{1,0:T(8,128)(2,1)} %bitcast.4, f32[1,2560]{1,0:T(1,128)} %bias.1, bf16[2048,256]{1,0:T(8,128)(2,1)} %bitcast.7, s32[1,128]{1,0:T(1,128)} %seg.1, s32[1,2]{1,0:T(1,128)} %start.1, s32[1,2]{1,0:T(1,128)} %height.1, ...), custom_call_target="tpu_custom_call" | custom-call | tf_op jit(solution)/shard_map/sublayers/pallas_call | solution.py:483
  148.9 2.3 %copy.12 = bf16[1,1,128,4096]{3,2,1,0:T(8,128)(2,1)} copy(bf16[1,1,128,4096]{3,2,1,0:T(8,128)(2,1)} %bitcast.5) | data formatting | bytes 2097152

commit v2 on v1

v2 whole, which is shorter than its diff:
```python
import math

import jax
import jax.numpy as jnp
from jax import lax
from jax.experimental import pallas as pl
from jax.experimental.pallas import tpu as pltpu
from jax.sharding import PartitionSpec as P

HD = 128
SEQ = 128
D = 8192
HALF = 4096
QUERY = 2048
CHUNK = 256
CHUNKS = 10
SLOTS = 8
EARLY = 4
PIECES = 4
PIECE = 512
GROUP = 8
BLOCK = 256
THETA = 1000000.0
EPSILON = 1e-06
MIB = 1 << 20
MESH = pl.DeviceIdType.MESH


def copy_to(src, dst, send, recv, device):
    return pltpu.make_async_remote_copy(
        src_ref=src,
        dst_ref=dst,
        send_sem=send,
        recv_sem=recv,
        device_id=device,
        device_id_type=MESH,
    )


def rotary_tables(seg_ref, start_ref, height_ref, width_ref, count_ref):
    row = lax.broadcasted_iota(jnp.int32, (SEQ, SEQ), 0)
    lane = lax.broadcasted_iota(jnp.int32, (SEQ, SEQ), 1)
    seg_keys = jnp.broadcast_to(seg_ref[...].astype(jnp.float32), (SEQ, SEQ))
    seg = jnp.sum(jnp.where(row == lane, seg_keys, 0.0), axis=1, keepdims=True)
    seg = jnp.broadcast_to(seg, (SEQ, SEQ))
    allowed = (row >= lane) & (seg == seg_keys)
    border = jnp.sum(jnp.where(seg_keys == 0.0, 1.0, 0.0), axis=1, keepdims=True)
    first = seg == 0.0

    def choose(ref):
        return jnp.where(
            first, ref[0, 0].astype(jnp.float32), ref[0, 1].astype(jnp.float32)
        )

    begin = jnp.where(first, 0.0, border)
    anchor = choose(start_ref)
    tall = choose(height_ref)
    broad = choose(width_ref)
    present = choose(count_ref)
    counter = row.astype(jnp.float32)
    span = tall * broad * present
    offset = counter - anchor
    inside = (offset >= 0.0) & (offset < span)
    relative = counter - begin
    shifted = relative - span + present * jnp.maximum(tall, broad)
    text = jnp.where(offset >= span, shifted, relative)
    base = anchor - begin
    clipped = jnp.maximum(offset, 0.0)
    grid_row = jnp.floor((clipped + 0.5) / broad)
    grid_col = clipped - grid_row * broad
    freq = lane % (HD // 2)
    inverse = jnp.exp(freq.astype(jnp.float32) * (-2.0 * math.log(THETA) / HD))
    moved = jnp.where(
        freq < HD // 8, 0.0, jnp.where(freq < HD // 8 + 3 * HD // 16, grid_row, grid_col)
    )
    angles = jnp.where(inside, base + moved, text) * inverse
    sine = jnp.sin(angles)
    return jnp.cos(angles), jnp.where(lane < HD // 2, -sine, sine), allowed


def kernel(
    hidden,
    gain,
    qkv,
    bias,
    out_weight,
    seg,
    start,
    height,
    width,
    count,
    out,
    wbuf,
    gathered,
    weights,
    scaled,
    squares,
    x_own,
    x_in,
    x_relay,
    total,
    part_out,
    part_in,
    sums,
    landed,
    projected,
    cosine,
    sine,
    mask,
    rows,
    keys,
    values,
    w_sem,
    local_sem,
    ws,
    wr,
    a_s,
    a_r,
    x_s,
    x_r,
    p_s,
    p_r,
    c_s,
    c_r,
    r_s,
    r_r,
    f_s,
    f_r,
):
    p = lax.axis_index("pipe")
    d = lax.axis_index("dp")
    t = lax.axis_index("tensor")
    xl = d % 2
    y = (d // 2) % 4
    z = d // 8

    def at(y_, xl_):
        return (y_ % 4) * 2 + xl_

    def device(slot, pipe=p, z_=z):
        return (pipe, (z_ % 4) * 8 + slot, t)

    own = at(y, xl)
    other_core = (p, d, 1 - t)
    partner = device(at(y, 1 - xl))
    y_up, y_down = device(at(y + 1, xl)), device(at(y + 3, xl))
    z_up, z_down = device(own, z_=z + 1), device(own, z_=z + 3)
    across = device(at(y, 1 - xl), pipe=1 - p)

    def weight_copy(step):
        chunk = (step + 8) % CHUNKS
        slot = step % SLOTS
        return pltpu.make_async_copy(
            qkv.at[:, pl.ds(pl.multiple_of(chunk * CHUNK, CHUNK), CHUNK)],
            wbuf.at[slot],
            w_sem.at[slot],
        )

    load_hidden = pltpu.make_async_copy(hidden, x_in, local_sem.at[PIECES])

    @pl.when(p == 0)
    def _():
        load_hidden.start()

    for step in range(SLOTS):
        weight_copy(step).start()
    own_weights = [
        pltpu.make_async_copy(
            out_weight.at[pl.ds(k * PIECE, PIECE)], weights.at[z, k], local_sem.at[k]
        )
        for k in range(PIECES)
    ]

    barrier = pltpu.get_barrier_semaphore()
    pl.semaphore_signal(barrier, inc=1, device_id=other_core, device_id_type=MESH)
    for to in (z_up, z_down):
        pl.semaphore_signal(barrier, inc=1, device_id=to, device_id_type=MESH)
    for j in range(GROUP):
        slot = (own + j) % GROUP
        pl.semaphore_signal(
            barrier, inc=1, device_id=device(slot, pipe=1 - p), device_id_type=MESH
        )
        if j:
            pl.semaphore_signal(barrier, inc=1, device_id=device(slot), device_id_type=MESH)

    def weight_up(k):
        src = out_weight.at[pl.ds(k * PIECE, PIECE)]
        return copy_to(src, weights.at[z, k], ws.at[0, k], wr.at[0, k], z_up)

    def weight_down(k):
        src = out_weight.at[pl.ds(k * PIECE, PIECE)]
        return copy_to(src, weights.at[z, k], ws.at[1, k], wr.at[1, k], z_down)

    def weight_pass_up(k):
        ref = weights.at[(z + 3) % 4, k, pl.ds(0, PIECE // 2)]
        return copy_to(ref, ref, ws.at[2, k], wr.at[2, k], z_up)

    def weight_pass_down(k):
        ref = weights.at[(z + 1) % 4, k, pl.ds(PIECE // 2, PIECE // 2)]
        return copy_to(ref, ref, ws.at[3, k], wr.at[3, k], z_down)

    def pass_weights(k):
        weight_up(k).wait_recv()
        weight_pass_up(k).start()
        weight_down(k).wait_recv()
        weight_pass_down(k).start()

    half = SEQ // 2

    def rows_copy(k, kind):
        ref, to = {
            0: (gathered.at[k, own], partner),
            1: (gathered.at[k, own], y_up),
            2: (gathered.at[k, own], y_down),
            3: (gathered.at[k, at(y, 1 - xl)], y_up),
            4: (gathered.at[k, at(y, 1 - xl)], y_down),
            5: (gathered.at[k, at(y + 3, xl), pl.ds(0, half)], y_up),
            6: (gathered.at[k, at(y + 1, xl), pl.ds(half, half)], y_down),
            7: (gathered.at[k, at(y + 2, xl)], partner),
        }[kind]
        return copy_to(ref, ref, a_s.at[kind, k], a_r.at[kind, k], to)

    def inject(k):
        for kind in (1, 2, 0):
            rows_copy(k, kind).start()

    def pass_first(k):
        rows_copy(k, 0).wait_recv()
        rows_copy(k, 3).start()
        rows_copy(k, 4).start()
        rows_copy(k, 1).wait_recv()
        rows_copy(k, 5).start()
        rows_copy(k, 2).wait_recv()
        rows_copy(k, 6).start()

    def pass_second(k):
        rows_copy(k, 5).wait_recv()
        rows_copy(k, 6).wait_recv()
        rows_copy(k, 7).start()

    def strip(k):
        return pl.ds(k * (SEQ // PIECES), SEQ // PIECES)

    def send_across(src, k):
        return copy_to(src.at[strip(k)], x_relay.at[strip(k)], r_s.at[k], r_r.at[k], across)

    def pass_across(dst, k):
        return copy_to(x_relay.at[strip(k)], dst.at[strip(k)], f_s.at[k], f_r.at[k], partner)

    cos, sin, allowed = rotary_tables(seg, start, height, width, count)
    cosine[...] = cos
    sine[...] = sin
    mask[...] = jnp.where(allowed, 1.0, 0.0)
    squares[t] = jnp.zeros((SEQ, 128), jnp.float32)

    def block(slot, zz):
        return pl.ds(pl.multiple_of(zz * 2048 + slot * BLOCK, BLOCK), BLOCK)

    def prepare(slot, zz, update):
        cols = block(slot, zz)
        x = x_in[:, cols]
        if update:
            x = x.astype(jnp.float32) + landed[0, slot, zz].astype(jnp.float32)
            x = x.astype(jnp.bfloat16)
        x_own[:, cols] = x
        x = x.astype(jnp.float32)
        g = gain[:, pl.ds(pl.multiple_of(t * HALF + zz * 2048 + slot * BLOCK, BLOCK), BLOCK)]
        scaled[t, :, cols] = (x * g).astype(jnp.bfloat16)
        x = x * x
        squares[t] += x[:, 0:128] + x[:, 128:256]

    def scaled_copy(slot, zz):
        ref = scaled.at[t, :, block(slot, zz)]
        return copy_to(ref, ref, x_s.at[slot, zz], x_r.at[slot, zz], other_core)

    squares_copy = copy_to(
        squares.at[t], squares.at[t], x_s.at[GROUP, 0], x_r.at[GROUP, 0], other_core
    )

    def landed_wait(layer, slot, zz):
        ref = landed.at[layer, slot, zz]
        pltpu.make_async_copy(ref, ref, c_r.at[layer, slot, zz]).wait()

    def rotated(u):
        return (u * cosine[...] + pltpu.roll(u, HD // 2, 1) * sine[...]).astype(jnp.bfloat16)

    def product(step, core):
        return jnp.dot(
            scaled[core],
            wbuf[step % SLOTS, pl.ds(pl.multiple_of(core * HALF, HALF), HALF)],
            preferred_element_type=jnp.float32,
        )

    def finished(step, u):
        cols = pl.ds(pl.multiple_of(((step + 8) % CHUNKS) * CHUNK, CHUNK), CHUNK)
        scale = rows[...]
        for h in range(2):
            lanes = slice(h * HD, (h + 1) * HD)
            projected[step, :, lanes] = u[:, lanes] * scale + bias[:, cols][:, lanes]

    def first_half(step, carry):
        weight_copy(step).wait()
        projected[step] = product(step, t)
        return carry

    def second_half(step, carry):
        finished(step, projected[step] + product(step, 1 - t))

        @pl.when(step + SLOTS < CHUNKS)
        def _():
            weight_copy(step + SLOTS).start()

        return carry

    @pl.when(p == 0)
    def _():
        load_hidden.wait()

        def body(slot, carry):
            for zz in range(2):
                prepare(slot, zz, False)
            return carry

        lax.fori_loop(0, GROUP, body, 0)
        lax.fori_loop(0, EARLY, first_half, 0)

    pl.semaphore_wait(barrier, 2 * GROUP + 2)

    @pl.when(p == 0)
    def _():
        for slot in range(GROUP):
            for zz in range(2):
                scaled_copy(slot, zz).start()
        squares_copy.start()

    for k in range(PIECES):
        weight_up(k).start()
        weight_down(k).start()
    for copy in own_weights:
        copy.start()

    @pl.when(p == 0)
    def _():
        for k in range(PIECES):
            send_across(hidden, k).start()

    @pl.when(p == 1)
    def _():
        for k in range(PIECES):
            pass_weights(k)
            send_across(hidden, k).wait_recv()
            pass_across(x_in, k).start()
        for k in range(PIECES):
            pass_across(x_in, k).wait_recv()

        def body(j, carry):
            slot = (own + j) % GROUP
            for zz in range(2):
                landed_wait(0, slot, zz)
                prepare(slot, zz, True)
                scaled_copy(slot, zz).start()
            return carry

        lax.fori_loop(0, GROUP, body, 0)
        squares_copy.start()
        for k in range(PIECES):
            send_across(x_own, k).start()

    lax.fori_loop(EARLY * (1 - p), SLOTS, first_half, 0)
    squares_copy.wait_recv()
    for slot in range(GROUP):
        for zz in range(2):
            scaled_copy(slot, zz).wait_recv()
    mean = jnp.sum(squares[0] + squares[1], axis=1, keepdims=True) * (1.0 / D)
    rows[...] = jnp.broadcast_to(lax.rsqrt(mean + EPSILON), (SEQ, SEQ))
    lax.fori_loop(0, 3, second_half, 0)
    for h in range(2):
        keys[h] = rotated(projected[0, :, h * HD : (h + 1) * HD])
        values[h] = projected[1, :, h * HD : (h + 1) * HD].astype(jnp.bfloat16)

    def attend(step):
        q_chunk = step - 2
        kv = q_chunk // 4
        for h in range(2):
            scores = lax.dot_general(
                rotated(projected[step, :, h * HD : (h + 1) * HD]),
                keys[kv],
                (((1,), (1,)), ((), ())),
                preferred_element_type=jnp.float32,
            ) * (1.0 / math.sqrt(HD))
            exponent = jnp.where(mask[...] > 0.0, jnp.exp(scores), 0.0)
            weight = exponent * (1.0 / jnp.sum(exponent, axis=1, keepdims=True))
            attended = jnp.dot(
                weight.astype(jnp.bfloat16), values[kv], preferred_element_type=jnp.float32
            )
            cols = pl.multiple_of((q_chunk % 2) * CHUNK + h * HD, HD)
            gathered[q_chunk // 2, own, :, pl.ds(cols, HD)] = attended.astype(jnp.bfloat16)

    def pass_on(q_chunk):
        @pl.when(q_chunk % 2 == 1)
        def _():
            inject(q_chunk // 2)

    def project_second(step, carry):
        attend(step - 1)
        finished(step, projected[step] + product(step, 1 - t))
        pass_on(step - 3)
        return carry

    def project_both(step, carry):
        weight_copy(step).wait()
        attend(step - 1)
        finished(step, product(step, 0) + product(step, 1))
        pass_on(step - 3)
        return carry

    lax.fori_loop(3, SLOTS, project_second, 0)
    lax.fori_loop(SLOTS, CHUNKS, project_both, 0)
    attend(CHUNKS - 1)
    inject(PIECES - 1)

    def part_copy(slot, zz):
        return copy_to(
            part_out.at[slot, zz],
            part_in.at[slot, zz],
            p_s.at[slot, zz],
            p_r.at[slot, zz],
            other_core,
        )

    def sums_copy(slot, zz):
        return copy_to(
            sums.at[slot, zz],
            landed.at[p, own, zz],
            c_s.at[slot, zz],
            c_r.at[p, own, zz],
            device(slot, pipe=1),
        )

    def nth(j):
        pair, odd = j // 2, j % 2
        along = (pair * (3 - pair)) // 2
        dy = along * (3 + 2 * odd) + 2 * (pair // 3)
        dx = (1 - along) * odd + (pair // 2) * (1 - pair // 3)
        return at(y + dy, (xl + dx) % 2)

    def unit(slot, zb):
        part = jnp.dot(gathered[0, slot], weights[zb, 0], preferred_element_type=jnp.float32)
        for k in range(1, PIECES):
            part += jnp.dot(gathered[k, slot], weights[zb, k], preferred_element_type=jnp.float32)

        @pl.when(zb // 2 == t)
        def _():
            total[slot, zb % 2] = part

        @pl.when(zb // 2 != t)
        def _():
            part_out[slot, zb % 2] = part.astype(jnp.bfloat16)
            part_copy(slot, zb % 2).start()

    def finish(slot, zb):
        zz = zb % 2

        @pl.when(zb // 2 == t)
        def _():
            part_copy(slot, zz).wait_recv()
            sums[slot, zz] = (total[slot, zz] + part_in[slot, zz].astype(jnp.float32)).astype(
                jnp.bfloat16
            )

            @pl.when((p == 0) | (slot != own))
            def _():
                sums_copy(slot, zz).start()

    def each(action, count, place):
        def body(i, carry):
            j, turn = place(i)
            action(nth(j), (z + turn) % 4)
            return carry

        lax.fori_loop(0, count, body, 0)

    def near(i):
        return i, 0

    def beside(i):
        return i // 2, 1 + 2 * (i % 2)

    def corner(i):
        return 4 + i // 3, i % 3 + (i % 3) // 2

    def facing(i):
        return 6, i + i // 2

    def far(i):
        return i, 2

    def last(i):
        return 7, i

    def pass_weights_now(k):
        @pl.when(p == 0)
        def _():
            pass_weights(k)

    pass_first(0)
    pass_weights_now(0)
    pass_first(1)
    pass_first(2)
    pass_weights_now(1)
    pass_first(3)
    for copy in own_weights:
        copy.wait()
    each(unit, 4, near)
    pass_weights_now(2)
    pass_second(0)
    each(finish, 4, near)
    pass_second(1)
    pass_weights_now(3)
    each(unit, 8, beside)
    pass_second(2)
    each(finish, 8, beside)
    pass_second(3)
    for k in range(PIECES):
        rows_copy(k, 3).wait_recv()
        rows_copy(k, 4).wait_recv()
    each(unit, 6, corner)
    each(finish, 6, corner)
    each(unit, 3, facing)
    each(finish, 3, facing)
    for k in range(PIECES):
        weight_pass_up(k).wait_recv()
        weight_pass_down(k).wait_recv()
    each(unit, 7, far)
    each(finish, 7, far)
    for k in range(PIECES):
        rows_copy(k, 7).wait_recv()
    each(unit, 4, last)
    each(finish, 4, last)

    @pl.when(p == 0)
    def _():
        for k in range(PIECES):
            send_across(x_own, k).wait_recv()
            pass_across(out, k).start()
        for slot in range(GROUP):
            for zz in range(2):
                sums_copy(slot, zz).wait_send()
        for k in range(PIECES):
            send_across(hidden, k).wait_send()
            pass_across(out, k).wait()

    @pl.when(p == 1)
    def _():
        def add(slot, zz, update):
            cols = block(slot, zz)
            out[:, cols] = (
                x_own[:, cols].astype(jnp.float32) + update.astype(jnp.float32)
            ).astype(jnp.bfloat16)

        def body(j, carry):
            slot = nth(j)
            for zz in range(2):
                landed_wait(1, slot, zz)
                add(slot, zz, landed[1, slot, zz])
            return carry

        for zz in range(2):
            add(own, zz, sums[own, zz])
        lax.fori_loop(1, GROUP, body, 0)
        for j in range(1, GROUP):
            for zz in range(2):
                sums_copy((own + j) % GROUP, zz).wait_send()
        for k in range(PIECES):
            send_across(x_own, k).wait_send()
            pass_across(x_in, k).wait_send()

    for k in range(PIECES):
        for copy in (weight_up(k), weight_down(k), weight_pass_up(k), weight_pass_down(k)):
            copy.wait_send()
        for kind in range(8):
            rows_copy(k, kind).wait_send()
    squares_copy.wait_send()
    for slot in range(GROUP):
        for zz in range(2):
            scaled_copy(slot, zz).wait_send()
            part_copy(slot, zz).wait_send()


def local(hidden, gain, qkv, bias, out_weight, segment, start, height, width, count):
    bf16, f32 = jnp.bfloat16, jnp.float32
    anywhere = pl.BlockSpec(memory_space=pl.ANY)
    vmem = pl.BlockSpec(memory_space=pltpu.VMEM)
    smem = pl.BlockSpec(memory_space=pltpu.SMEM)
    dma = pltpu.SemaphoreType.DMA
    result = pl.pallas_call(
        kernel,
        out_shape=jax.ShapeDtypeStruct((SEQ, HALF), bf16),
        in_specs=[anywhere, vmem, anywhere, vmem, anywhere, vmem, smem, smem, smem, smem],
        out_specs=vmem,
        scratch_shapes=[
            pltpu.VMEM((SLOTS, D, CHUNK), bf16),
            pltpu.VMEM((PIECES, GROUP, SEQ, PIECE), bf16),
            pltpu.VMEM((4, PIECES, PIECE, BLOCK), bf16),
            pltpu.VMEM((2, SEQ, HALF), bf16),
            pltpu.VMEM((2, SEQ, 128), f32),
            pltpu.VMEM((SEQ, HALF), bf16),
            pltpu.VMEM((SEQ, HALF), bf16),
            pltpu.VMEM((SEQ, HALF), bf16),
            pltpu.VMEM((GROUP, 2, SEQ, BLOCK), f32),
            pltpu.VMEM((GROUP, 2, SEQ, BLOCK), bf16),
            pltpu.VMEM((GROUP, 2, SEQ, BLOCK), bf16),
            pltpu.VMEM((GROUP, 2, SEQ, BLOCK), bf16),
            pltpu.VMEM((2, GROUP, 2, SEQ, BLOCK), bf16),
            pltpu.VMEM((CHUNKS, SEQ, CHUNK), f32),
            pltpu.VMEM((SEQ, SEQ), f32),
            pltpu.VMEM((SEQ, SEQ), f32),
            pltpu.VMEM((SEQ, SEQ), f32),
            pltpu.VMEM((SEQ, SEQ), f32),
            pltpu.VMEM((2, SEQ, HD), bf16),
            pltpu.VMEM((2, SEQ, HD), bf16),
            dma((SLOTS,)),
            dma((PIECES + 1,)),
            dma((4, PIECES)),
            dma((4, PIECES)),
            dma((8, PIECES)),
            dma((8, PIECES)),
            dma((GROUP + 1, 2)),
            dma((GROUP + 1, 2)),
            dma((GROUP, 2)),
            dma((GROUP, 2)),
            dma((GROUP, 2)),
            dma((2, GROUP, 2)),
            dma((PIECES,)),
            dma((PIECES,)),
            dma((PIECES,)),
            dma((PIECES,)),
        ],
        compiler_params=pltpu.CompilerParams(
            collective_id=0, has_side_effects=True, vmem_limit_bytes=61 * MIB
        ),
        name="sublayers",
    )(
        hidden[0],
        gain,
        qkv[0],
        bias,
        out_weight[0],
        segment,
        start,
        height,
        width,
        count,
    )
    return result[None, None]


def solution(mesh):
    return jax.shard_map(
        local,
        mesh=mesh,
        in_specs=(
            P(None, "dp", "tensor"),
            P("pipe", None),
            P("pipe", None, "tensor"),
            P("pipe", "tensor"),
            P("pipe", "tensor", "dp"),
            P(None, "dp"),
            P(None, "dp"),
            P(None, "dp"),
            P(None, "dp"),
            P(None, "dp"),
        ),
        out_specs=P("pipe", None, "dp", "tensor"),
        check_vma=False,
    )
```

time: 151 us -> 131 us (0.87)
  Pallas kernels: 149 us -> 129 us
    pallas_call x1, Pallas kernels: 149 us -> 129 us  [local(): pl.pallas_call(kernel, out_shape=jax.ShapeDtypeStruct((SEQ, HALF), bf16),...]
where the time goes in v2:
time: 131 us
  Pallas kernels  129 us (98%)
  local copies, waits for them, and re-layouts  2.29 us (2%)
    pallas_call x1, Pallas kernels, local(): pl.pallas_call(kernel, out_shape=jax.ShapeDtypeStruct((SEQ, HALF), bf16),...  129 us

profile of v2, /device:TPU:7, one launch (start us, length us, event | category | flops | bytes accessed | tf_op | source)
XLA Modules:
  0.0 131.0 jit_solution(7482194269980007470)
XLA Ops:
  0.0 128.7 %sublayers.1 = bf16[128,4096]{1,0:T(8,128)(2,1)} custom-call(bf16[128,4096]{1,0:T(8,128)(2,1)} %bitcast.6, f32[1,8192]{1,0:T(1,128)} %gain.1, bf16[8192,2560]{1,0:T(8,128)(2,1)} %bitcast.4, f32[1,2560]{1,0:T(1,128)} %bias.1, bf16[2048,256]{1,0:T(8,128)(2,1)} %bitcast.7, s32[1,128]{1,0:T(1,128)} %seg.1, s32[1,2]{1,0:T(1,128)} %start.1, s32[1,2]{1,0:T(1,128)} %height.1, ...), custom_call_target="tpu_custom_call" | custom-call | tf_op jit(solution)/shard_map/sublayers/pallas_call | solution.py:596
  128.7 2.3 %copy.12 = bf16[1,1,128,4096]{3,2,1,0:T(8,128)(2,1)} copy(bf16[1,1,128,4096]{3,2,1,0:T(8,128)(2,1)} %bitcast.5) | data formatting | bytes 2097152

commit v3 on v2

--- a/solution.py
+++ b/solution.py
@@ -162,11 +162,11 @@
     def _():
         load_hidden.start()
 
-    for step in range(SLOTS):
+    for step in range(EARLY):
         weight_copy(step).start()
     own_weights = [
         pltpu.make_async_copy(
-            out_weight.at[pl.ds(k * PIECE, PIECE)], weights.at[z, k], local_sem.at[k]
+            out_weight.at[pl.ds(k * PIECE, PIECE)], weights.at[xl, z, k], local_sem.at[k]
         )
         for k in range(PIECES)
     ]
@@ -185,19 +185,31 @@
 
     def weight_up(k):
         src = out_weight.at[pl.ds(k * PIECE, PIECE)]
-        return copy_to(src, weights.at[z, k], ws.at[0, k], wr.at[0, k], z_up)
+        return copy_to(src, weights.at[xl, z, k], ws.at[0, k], wr.at[0, k], z_up)
 
     def weight_down(k):
         src = out_weight.at[pl.ds(k * PIECE, PIECE)]
-        return copy_to(src, weights.at[z, k], ws.at[1, k], wr.at[1, k], z_down)
+        return copy_to(src, weights.at[xl, z, k], ws.at[1, k], wr.at[1, k], z_down)
 
     def weight_pass_up(k):
-        ref = weights.at[(z + 3) % 4, k, pl.ds(0, PIECE // 2)]
+        ref = weights.at[xl, (z + 3) % 4, k, pl.ds(0, PIECE // 2)]
         return copy_to(ref, ref, ws.at[2, k], wr.at[2, k], z_up)
 
     def weight_pass_down(k):
-        ref = weights.at[(z + 1) % 4, k, pl.ds(PIECE // 2, PIECE // 2)]
+        ref = weights.at[xl, (z + 1) % 4, k, pl.ds(PIECE // 2, PIECE // 2)]
         return copy_to(ref, ref, ws.at[3, k], wr.at[3, k], z_down)
+
+    def weight_over(k):
+        src = out_weight.at[pl.ds(k * PIECE, PIECE)]
+        return copy_to(src, weights.at[xl, z, k], ws.at[4, k], wr.at[4, k], partner)
+
+    def weight_on(k, kind):
+        ref = weights.at[1 - xl, z, k]
+        return copy_to(ref, ref, ws.at[kind, k], wr.at[kind, k], z_up if kind == 5 else z_down)
+
+    def weight_opposite(k):
+        ref = weights.at[xl, (z + 2) % 4, k]
+        return copy_to(ref, ref, ws.at[7, k], wr.at[7, k], partner)
 
     def pass_weights(k):
         weight_up(k).wait_recv()
@@ -221,13 +233,20 @@
         return copy_to(ref, ref, a_s.at[kind, k], a_r.at[kind, k], to)
 
     def inject(k):
-        for kind in (1, 2, 0):
+        for kind in (1, 2):
             rows_copy(k, kind).start()
+
+        @pl.when(p == 0)
+        def _():
+            rows_copy(k, 0).start()
 
     def pass_first(k):
         rows_copy(k, 0).wait_recv()
         rows_copy(k, 3).start()
         rows_copy(k, 4).start()
+        pass_along(k)
+
+    def pass_along(k):
         rows_copy(k, 1).wait_recv()
         rows_copy(k, 5).start()
         rows_copy(k, 2).wait_recv()
@@ -276,6 +295,9 @@
     squares_copy = copy_to(
         squares.at[t], squares.at[t], x_s.at[GROUP, 0], x_r.at[GROUP, 0], other_core
     )
+    scaled_whole = copy_to(
+        scaled.at[t], scaled.at[t], x_s.at[GROUP, 1], x_r.at[GROUP, 1], other_core
+    )
 
     def landed_wait(layer, slot, zz):
         ref = landed.at[layer, slot, zz]
@@ -328,14 +350,14 @@
 
     @pl.when(p == 0)
     def _():
-        for slot in range(GROUP):
-            for zz in range(2):
-                scaled_copy(slot, zz).start()
+        scaled_whole.start()
         squares_copy.start()
 
     for k in range(PIECES):
         weight_up(k).start()
         weight_down(k).start()
+    for step in range(EARLY, SLOTS):
+        weight_copy(step).start()
     for copy in own_weights:
         copy.start()
 
@@ -346,10 +368,19 @@
 
     @pl.when(p == 1)
     def _():
+        for k in range(PIECES):
+            weight_over(k).start()
         for k in range(PIECES):
             pass_weights(k)
             send_across(hidden, k).wait_recv()
             pass_across(x_in, k).start()
+            weight_over(k).wait_recv()
+            weight_on(k, 5).start()
+            weight_on(k, 6).start()
+        for k in range(PIECES):
+            weight_pass_up(k).wait_recv()
+            weight_pass_down(k).wait_recv()
+            weight_opposite(k).start()
         for k in range(PIECES):
             pass_across(x_in, k).wait_recv()
 
@@ -368,9 +399,17 @@
 
     lax.fori_loop(EARLY * (1 - p), SLOTS, first_half, 0)
     squares_copy.wait_recv()
-    for slot in range(GROUP):
-        for zz in range(2):
-            scaled_copy(slot, zz).wait_recv()
+
+    @pl.when(p == 0)
+    def _():
+        scaled_whole.wait_recv()
+
+    @pl.when(p == 1)
+    def _():
+        for slot in range(GROUP):
+            for zz in range(2):
+                scaled_copy(slot, zz).wait_recv()
+
     mean = jnp.sum(squares[0] + squares[1], axis=1, keepdims=True) * (1.0 / D)
     rows[...] = jnp.broadcast_to(lax.rsqrt(mean + EPSILON), (SEQ, SEQ))
     lax.fori_loop(0, 3, second_half, 0)
@@ -419,22 +458,24 @@
     attend(CHUNKS - 1)
     inject(PIECES - 1)
 
-    def part_copy(slot, zz):
+    def stream_of(e):
+        return e + p * (xl - e % 2)
+
+    def place_of(e):
+        return own + p * (e % 2 - xl)
+
+    def part_copy(e, zz):
         return copy_to(
-            part_out.at[slot, zz],
-            part_in.at[slot, zz],
-            p_s.at[slot, zz],
-            p_r.at[slot, zz],
-            other_core,
+            part_out.at[e, zz], part_in.at[e, zz], p_s.at[e, zz], p_r.at[e, zz], other_core
         )
 
-    def sums_copy(slot, zz):
+    def sums_copy(e, zz):
         return copy_to(
-            sums.at[slot, zz],
-            landed.at[p, own, zz],
-            c_s.at[slot, zz],
-            c_r.at[p, own, zz],
-            device(slot, pipe=1),
+            sums.at[e, zz],
+            landed.at[p, place_of(e), zz],
+            c_s.at[e, zz],
+            c_r.at[p, place_of(e), zz],
+            device(stream_of(e), pipe=1),
         )
 
     def nth(j):
@@ -444,33 +485,34 @@
         dx = (1 - along) * odd + (pair // 2) * (1 - pair // 3)
         return at(y + dy, (xl + dx) % 2)
 
-    def unit(slot, zb):
-        part = jnp.dot(gathered[0, slot], weights[zb, 0], preferred_element_type=jnp.float32)
+    def unit(e, zb):
+        stream, xb = stream_of(e), xl + p * (e % 2 - xl)
+        part = jnp.dot(gathered[0, stream], weights[xb, zb, 0], preferred_element_type=jnp.float32)
         for k in range(1, PIECES):
-            part += jnp.dot(gathered[k, slot], weights[zb, k], preferred_element_type=jnp.float32)
+            part += jnp.dot(
+                gathered[k, stream], weights[xb, zb, k], preferred_element_type=jnp.float32
+            )
 
         @pl.when(zb // 2 == t)
         def _():
-            total[slot, zb % 2] = part
+            total[e, zb % 2] = part
 
         @pl.when(zb // 2 != t)
         def _():
-            part_out[slot, zb % 2] = part.astype(jnp.bfloat16)
-            part_copy(slot, zb % 2).start()
-
-    def finish(slot, zb):
+            part_out[e, zb % 2] = part.astype(jnp.bfloat16)
+            part_copy(e, zb % 2).start()
+
+    def finish(e, zb):
         zz = zb % 2
 
         @pl.when(zb // 2 == t)
         def _():
-            part_copy(slot, zz).wait_recv()
-            sums[slot, zz] = (total[slot, zz] + part_in[slot, zz].astype(jnp.float32)).astype(
-                jnp.bfloat16
-            )
-
-            @pl.when((p == 0) | (slot != own))
+            part_copy(e, zz).wait_recv()
+            sums[e, zz] = (total[e, zz] + part_in[e, zz].astype(jnp.float32)).astype(jnp.bfloat16)
+
+            @pl.when((p == 0) | (e // 2 != y))
             def _():
-                sums_copy(slot, zz).start()
+                sums_copy(e, zz).start()
 
     def each(action, count, place):
         def body(i, carry):
@@ -480,6 +522,13 @@
 
         lax.fori_loop(0, count, body, 0)
 
+    def each_along(action, dy):
+        def body(i, carry):
+            action(at(y + dy, (xl + i // 4) % 2), (z + i % 4) % 4)
+            return carry
+
+        lax.fori_loop(0, 8, body, 0)
+
     def near(i):
         return i, 0
 
@@ -498,57 +547,78 @@
     def last(i):
         return 7, i
 
-    def pass_weights_now(k):
-        @pl.when(p == 0)
-        def _():
-            pass_weights(k)
-
-    pass_first(0)
-    pass_weights_now(0)
-    pass_first(1)
-    pass_first(2)
-    pass_weights_now(1)
-    pass_first(3)
     for copy in own_weights:
         copy.wait()
-    each(unit, 4, near)
-    pass_weights_now(2)
-    pass_second(0)
-    each(finish, 4, near)
-    pass_second(1)
-    pass_weights_now(3)
-    each(unit, 8, beside)
-    pass_second(2)
-    each(finish, 8, beside)
-    pass_second(3)
-    for k in range(PIECES):
-        rows_copy(k, 3).wait_recv()
-        rows_copy(k, 4).wait_recv()
-    each(unit, 6, corner)
-    each(finish, 6, corner)
-    each(unit, 3, facing)
-    each(finish, 3, facing)
-    for k in range(PIECES):
-        weight_pass_up(k).wait_recv()
-        weight_pass_down(k).wait_recv()
-    each(unit, 7, far)
-    each(finish, 7, far)
-    for k in range(PIECES):
-        rows_copy(k, 7).wait_recv()
-    each(unit, 4, last)
-    each(finish, 4, last)
+
+    @pl.when(p == 0)
+    def _():
+        pass_first(0)
+        pass_weights(0)
+        pass_first(1)
+        pass_first(2)
+        pass_weights(1)
+        pass_first(3)
+        each(unit, 4, near)
+        pass_weights(2)
+        pass_second(0)
+        each(finish, 4, near)
+        pass_second(1)
+        pass_weights(3)
+        each(unit, 8, beside)
+        pass_second(2)
+        each(finish, 8, beside)
+        pass_second(3)
+        for k in range(PIECES):
+            rows_copy(k, 3).wait_recv()
+            rows_copy(k, 4).wait_recv()
+        each(unit, 6, corner)
+        each(finish, 6, corner)
+        each(unit, 3, facing)
+        each(finish, 3, facing)
+        for k in range(PIECES):
+            weight_pass_up(k).wait_recv()
+            weight_pass_down(k).wait_recv()
+        each(unit, 7, far)
+        each(finish, 7, far)
+        for k in range(PIECES):
+            rows_copy(k, 7).wait_recv()
+        each(unit, 4, last)
+        each(finish, 4, last)
+
+    @pl.when(p == 1)
+    def _():
+        for k in range(PIECES):
+            pass_along(k)
+        for k in range(PIECES):
+            weight_on(k, 5).wait_recv()
+            weight_on(k, 6).wait_recv()
+            weight_opposite(k).wait_recv()
+        each_along(unit, 3)
+        each_along(finish, 3)
+        each_along(unit, 1)
+        each_along(finish, 1)
+        each_along(unit, 0)
+        for k in range(PIECES):
+            rows_copy(k, 5).wait_recv()
+            rows_copy(k, 6).wait_recv()
+        each_along(unit, 2)
+        each_along(finish, 2)
+        each_along(finish, 0)
 
     @pl.when(p == 0)
     def _():
         for k in range(PIECES):
             send_across(x_own, k).wait_recv()
             pass_across(out, k).start()
-        for slot in range(GROUP):
+        for e in range(GROUP):
             for zz in range(2):
-                sums_copy(slot, zz).wait_send()
+                sums_copy(e, zz).wait_send()
         for k in range(PIECES):
             send_across(hidden, k).wait_send()
             pass_across(out, k).wait()
+            for kind in (0, 3, 4, 7):
+                rows_copy(k, kind).wait_send()
+        scaled_whole.wait_send()
 
     @pl.when(p == 1)
     def _():
@@ -558,33 +628,40 @@
                 x_own[:, cols].astype(jnp.float32) + update.astype(jnp.float32)
             ).astype(jnp.bfloat16)
 
-        def body(j, carry):
-            slot = nth(j)
+        def body(i, carry):
+            slot = at(y + 1 + i // 2, i % 2)
             for zz in range(2):
                 landed_wait(1, slot, zz)
                 add(slot, zz, landed[1, slot, zz])
             return carry
 
-        for zz in range(2):
-            add(own, zz, sums[own, zz])
-        lax.fori_loop(1, GROUP, body, 0)
-        for j in range(1, GROUP):
+        for xb in range(2):
             for zz in range(2):
-                sums_copy((own + j) % GROUP, zz).wait_send()
+                add(at(y, xb), zz, sums[at(y, xb), zz])
+        lax.fori_loop(0, GROUP - 2, body, 0)
+        for j in range(2, GROUP):
+            for zz in range(2):
+                sums_copy((2 * y + j) % GROUP, zz).wait_send()
         for k in range(PIECES):
             send_across(x_own, k).wait_send()
             pass_across(x_in, k).wait_send()
+            weight_over(k).wait_send()
+            weight_on(k, 5).wait_send()
+            weight_on(k, 6).wait_send()
+            weight_opposite(k).wait_send()
+        for slot in range(GROUP):
+            for zz in range(2):
+                scaled_copy(slot, zz).wait_send()
 
     for k in range(PIECES):
         for copy in (weight_up(k), weight_down(k), weight_pass_up(k), weight_pass_down(k)):
             copy.wait_send()
-        for kind in range(8):
+        for kind in (1, 2, 5, 6):
             rows_copy(k, kind).wait_send()
     squares_copy.wait_send()
-    for slot in range(GROUP):
+    for e in range(GROUP):
         for zz in range(2):
-            scaled_copy(slot, zz).wait_send()
-            part_copy(slot, zz).wait_send()
+            part_copy(e, zz).wait_send()
 
 
 def local(hidden, gain, qkv, bias, out_weight, segment, start, height, width, count):
@@ -601,7 +678,7 @@
         scratch_shapes=[
             pltpu.VMEM((SLOTS, D, CHUNK), bf16),
             pltpu.VMEM((PIECES, GROUP, SEQ, PIECE), bf16),
-            pltpu.VMEM((4, PIECES, PIECE, BLOCK), bf16),
+            pltpu.VMEM((2, 4, PIECES, PIECE, BLOCK), bf16),
             pltpu.VMEM((2, SEQ, HALF), bf16),
             pltpu.VMEM((2, SEQ, 128), f32),
             pltpu.VMEM((SEQ, HALF), bf16),
@@ -621,8 +698,8 @@
             pltpu.VMEM((2, SEQ, HD), bf16),
             dma((SLOTS,)),
             dma((PIECES + 1,)),
-            dma((4, PIECES)),
-            dma((4, PIECES)),
+            dma((8, PIECES)),
+            dma((8, PIECES)),
             dma((8, PIECES)),
             dma((8, PIECES)),
             dma((GROUP + 1, 2)),

time: 131 us -> 120 us (0.916)
  Pallas kernels: 129 us -> 117 us
    pallas_call x1, Pallas kernels: 129 us -> 117 us  [local(): pl.pallas_call(kernel, out_shape=jax.ShapeDtypeStruct((SEQ, HALF), bf16),...]
where the time goes in v3:
time: 120 us
  Pallas kernels  117 us (98%)
  local copies, waits for them, and re-layouts  2.29 us (2%)
    pallas_call x1, Pallas kernels, local(): pl.pallas_call(kernel, out_shape=jax.ShapeDtypeStruct((SEQ, HALF), bf16),...  117 us

profile of v3, /device:TPU:7, one launch (start us, length us, event | category | flops | bytes accessed | tf_op | source)
XLA Modules:
  0.0 119.7 jit_solution(1030989800801833454)
XLA Ops:
  0.0 117.4 %sublayers.1 = bf16[128,4096]{1,0:T(8,128)(2,1)} custom-call(bf16[128,4096]{1,0:T(8,128)(2,1)} %bitcast.6, f32[1,8192]{1,0:T(1,128)} %gain.1, bf16[8192,2560]{1,0:T(8,128)(2,1)} %bitcast.4, f32[1,2560]{1,0:T(1,128)} %bias.1, bf16[2048,256]{1,0:T(8,128)(2,1)} %bitcast.7, s32[1,128]{1,0:T(1,128)} %seg.1, s32[1,2]{1,0:T(1,128)} %start.1, s32[1,2]{1,0:T(1,128)} %height.1, ...), custom_call_target="tpu_custom_call" | custom-call | tf_op jit(solution)/shard_map/sublayers/pallas_call | solution.py:673
  117.4 2.3 %copy.12 = bf16[1,1,128,4096]{3,2,1,0:T(8,128)(2,1)} copy(bf16[1,1,128,4096]{3,2,1,0:T(8,128)(2,1)} %bitcast.5) | data formatting | bytes 2097152

commit v4 on v3

--- a/solution.py
+++ b/solution.py
@@ -15,7 +15,8 @@
 CHUNK = 256
 CHUNKS = 10
 SLOTS = 8
-EARLY = 4
+EARLY = 1
+AHEAD = 2
 PIECES = 4
 PIECE = 512
 GROUP = 8
@@ -80,16 +81,24 @@
 
 def kernel(
     hidden,
+    gain_in,
+    qkv,
+    bias_in,
+    out_weight,
+    seg_in,
+    start_in,
+    height_in,
+    width_in,
+    count_in,
+    out,
     gain,
-    qkv,
     bias,
-    out_weight,
     seg,
     start,
     height,
     width,
     count,
-    out,
+    small_sem,
     wbuf,
     gathered,
     weights,
@@ -157,12 +166,28 @@
         )
 
     load_hidden = pltpu.make_async_copy(hidden, x_in, local_sem.at[PIECES])
+    small = [
+        pltpu.make_async_copy(src, dst, small_sem.at[i])
+        for i, (src, dst) in enumerate(
+            (
+                (seg_in, seg),
+                (start_in, start),
+                (height_in, height),
+                (width_in, width),
+                (count_in, count),
+                (gain_in, gain),
+                (bias_in, bias),
+            )
+        )
+    ]
+    for copy in small:
+        copy.start()
 
     @pl.when(p == 0)
     def _():
         load_hidden.start()
 
-    for step in range(EARLY):
+    for step in range(AHEAD):
         weight_copy(step).start()
     own_weights = [
         pltpu.make_async_copy(
@@ -266,6 +291,8 @@
     def pass_across(dst, k):
         return copy_to(x_relay.at[strip(k)], dst.at[strip(k)], f_s.at[k], f_r.at[k], partner)
 
+    for copy in small:
+        copy.wait()
     cos, sin, allowed = rotary_tables(seg, start, height, width, count)
     cosine[...] = cos
     sine[...] = sin
@@ -353,11 +380,11 @@
         scaled_whole.start()
         squares_copy.start()
 
+    for step in range(AHEAD, SLOTS):
+        weight_copy(step).start()
     for k in range(PIECES):
         weight_up(k).start()
         weight_down(k).start()
-    for step in range(EARLY, SLOTS):
-        weight_copy(step).start()
     for copy in own_weights:
         copy.start()
 
@@ -536,10 +563,10 @@
         return i // 2, 1 + 2 * (i % 2)
 
     def corner(i):
-        return 4 + i // 3, i % 3 + (i % 3) // 2
+        return 4 + i // 4, i % 4
 
     def facing(i):
-        return 6, i + i // 2
+        return 6, i
 
     def far(i):
         return i, 2
@@ -558,28 +585,28 @@
         pass_first(2)
         pass_weights(1)
         pass_first(3)
+        pass_weights(2)
         each(unit, 4, near)
-        pass_weights(2)
+        pass_weights(3)
+        each(finish, 4, near)
+        each(unit, 8, beside)
         pass_second(0)
-        each(finish, 4, near)
+        each(finish, 8, beside)
         pass_second(1)
-        pass_weights(3)
-        each(unit, 8, beside)
+        for k in range(PIECES):
+            weight_pass_up(k).wait_recv()
+            weight_pass_down(k).wait_recv()
+        each(unit, 4, far)
+        each(finish, 4, far)
         pass_second(2)
-        each(finish, 8, beside)
         pass_second(3)
         for k in range(PIECES):
             rows_copy(k, 3).wait_recv()
             rows_copy(k, 4).wait_recv()
-        each(unit, 6, corner)
-        each(finish, 6, corner)
-        each(unit, 3, facing)
-        each(finish, 3, facing)
-        for k in range(PIECES):
-            weight_pass_up(k).wait_recv()
-            weight_pass_down(k).wait_recv()
-        each(unit, 7, far)
-        each(finish, 7, far)
+        each(unit, 8, corner)
+        each(finish, 8, corner)
+        each(unit, 4, facing)
+        each(finish, 4, facing)
         for k in range(PIECES):
             rows_copy(k, 7).wait_recv()
         each(unit, 4, last)
@@ -587,17 +614,19 @@
 
     @pl.when(p == 1)
     def _():
-        for k in range(PIECES):
-            pass_along(k)
+        pass_along(0)
+        pass_along(1)
         for k in range(PIECES):
             weight_on(k, 5).wait_recv()
             weight_on(k, 6).wait_recv()
             weight_opposite(k).wait_recv()
+        each_along(unit, 0)
+        pass_along(2)
+        pass_along(3)
         each_along(unit, 3)
         each_along(finish, 3)
         each_along(unit, 1)
         each_along(finish, 1)
-        each_along(unit, 0)
         for k in range(PIECES):
             rows_copy(k, 5).wait_recv()
             rows_copy(k, 6).wait_recv()
@@ -668,14 +697,21 @@
     bf16, f32 = jnp.bfloat16, jnp.float32
     anywhere = pl.BlockSpec(memory_space=pl.ANY)
     vmem = pl.BlockSpec(memory_space=pltpu.VMEM)
-    smem = pl.BlockSpec(memory_space=pltpu.SMEM)
     dma = pltpu.SemaphoreType.DMA
     result = pl.pallas_call(
         kernel,
         out_shape=jax.ShapeDtypeStruct((SEQ, HALF), bf16),
-        in_specs=[anywhere, vmem, anywhere, vmem, anywhere, vmem, smem, smem, smem, smem],
+        in_specs=[anywhere] * 10,
         out_specs=vmem,
         scratch_shapes=[
+            pltpu.VMEM(gain.shape, f32),
+            pltpu.VMEM(bias.shape, f32),
+            pltpu.VMEM(segment.shape, jnp.int32),
+            pltpu.SMEM(start.shape, jnp.int32),
+            pltpu.SMEM(height.shape, jnp.int32),
+            pltpu.SMEM(width.shape, jnp.int32),
+            pltpu.SMEM(count.shape, jnp.int32),
+            dma((7,)),
             pltpu.VMEM((SLOTS, D, CHUNK), bf16),
             pltpu.VMEM((PIECES, GROUP, SEQ, PIECE), bf16),
             pltpu.VMEM((2, 4, PIECES, PIECE, BLOCK), bf16),

time: 120 us -> 113 us (0.942)
  Pallas kernels: 117 us -> 110 us
    pallas_call x1, Pallas kernels: 117 us -> 110 us  [local(): pl.pallas_call(kernel, out_shape=jax.ShapeDtypeStruct((SEQ, HALF), bf16),...]
where the time goes in v4:
time: 113 us
  Pallas kernels  110 us (97%)
  local copies, waits for them, and re-layouts  2.29 us (2%)
    pallas_call x1, Pallas kernels, local(): pl.pallas_call(kernel, out_shape=jax.ShapeDtypeStruct((SEQ, HALF), bf16),...  110 us
    unnamed x1, local copies, waits for them, and re-layouts  2.29 us

profile of v4, /device:TPU:7, one launch (start us, length us, event | category | flops | bytes accessed | tf_op | source)
XLA Modules:
  0.0 112.8 jit_solution(9049910517078902654)
XLA Ops:
  0.0 110.5 %sublayers.1 = bf16[128,4096]{1,0:T(8,128)(2,1)} custom-call(bf16[128,4096]{1,0:T(8,128)(2,1)} %bitcast.6, f32[1,8192]{1,0:T(1,128)} %gain_in.1, bf16[8192,2560]{1,0:T(8,128)(2,1)} %bitcast.4, f32[1,2560]{1,0:T(1,128)} %bias_in.1, bf16[2048,256]{1,0:T(8,128)(2,1)} %bitcast.7, s32[1,128]{1,0:T(1,128)} %seg_in.1, s32[1,2]{1,0:T(1,128)} %start_in.1, ...), custom_call_target="tpu_custom_call" | custom-call | tf_op jit(solution)/shard_map/sublayers/pallas_call | solution.py:701
  110.5 2.3 %copy.12 = bf16[1,1,128,4096]{3,2,1,0:T(8,128)(2,1)} copy(bf16[1,1,128,4096]{3,2,1,0:T(8,128)(2,1)} %bitcast.5) | data formatting | bytes 2097152

commit v5 on v4

--- a/solution.py
+++ b/solution.py
@@ -150,6 +150,14 @@
         return (pipe, (z_ % 4) * 8 + slot, t)
 
     own = at(y, xl)
+
+    def nth(j):
+        pair, odd = j // 2, j % 2
+        along = (pair * (3 - pair)) // 2
+        dy = along * (3 + 2 * odd) + 2 * (pair // 3)
+        dx = (1 - along) * odd + (pair // 2) * (1 - pair // 3)
+        return at(y + dy, (xl + dx) % 2)
+
     other_core = (p, d, 1 - t)
     partner = device(at(y, 1 - xl))
     y_up, y_down = device(at(y + 1, xl)), device(at(y + 3, xl))
@@ -361,6 +369,22 @@
 
         return carry
 
+    def accumulate(core, slot):
+        lhs = [scaled[core, :, block(slot, zz)] for zz in range(2)]
+        depth = [
+            pl.ds(pl.multiple_of(core * HALF + zz * 2048 + slot * BLOCK, BLOCK), BLOCK)
+            for zz in range(2)
+        ]
+        parts = [
+            [
+                jnp.dot(lhs[zz], wbuf[step, depth[zz]], preferred_element_type=jnp.float32)
+                for zz in range(2)
+            ]
+            for step in range(SLOTS)
+        ]
+        for step in range(SLOTS):
+            projected[step] += parts[step][0] + parts[step][1]
+
     @pl.when(p == 0)
     def _():
         load_hidden.wait()
@@ -411,38 +435,45 @@
         for k in range(PIECES):
             pass_across(x_in, k).wait_recv()
 
+        for step in range(SLOTS):
+            weight_copy(step).wait()
+            projected[step] = jnp.zeros((SEQ, CHUNK), jnp.float32)
+
+        def from_other(slot):
+            for zz in range(2):
+                scaled_copy(slot, zz).wait_recv()
+            accumulate(1 - t, slot)
+
         def body(j, carry):
-            slot = (own + j) % GROUP
+            slot = nth(j)
             for zz in range(2):
                 landed_wait(0, slot, zz)
                 prepare(slot, zz, True)
                 scaled_copy(slot, zz).start()
+            accumulate(t, slot)
+
+            @pl.when(j > 1)
+            def _():
+                from_other(nth(j - 2))
+
             return carry
 
         lax.fori_loop(0, GROUP, body, 0)
         squares_copy.start()
         for k in range(PIECES):
             send_across(x_own, k).start()
-
-    lax.fori_loop(EARLY * (1 - p), SLOTS, first_half, 0)
-    squares_copy.wait_recv()
-
-    @pl.when(p == 0)
-    def _():
-        scaled_whole.wait_recv()
-
-    @pl.when(p == 1)
-    def _():
-        for slot in range(GROUP):
-            for zz in range(2):
-                scaled_copy(slot, zz).wait_recv()
-
-    mean = jnp.sum(squares[0] + squares[1], axis=1, keepdims=True) * (1.0 / D)
-    rows[...] = jnp.broadcast_to(lax.rsqrt(mean + EPSILON), (SEQ, SEQ))
-    lax.fori_loop(0, 3, second_half, 0)
-    for h in range(2):
-        keys[h] = rotated(projected[0, :, h * HD : (h + 1) * HD])
-        values[h] = projected[1, :, h * HD : (h + 1) * HD].astype(jnp.bfloat16)
+        from_other(nth(GROUP - 2))
+        from_other(nth(GROUP - 1))
+
+    def row_scales():
+        squares_copy.wait_recv()
+        mean = jnp.sum(squares[0] + squares[1], axis=1, keepdims=True) * (1.0 / D)
+        rows[...] = jnp.broadcast_to(lax.rsqrt(mean + EPSILON), (SEQ, SEQ))
+
+    def keys_and_values():
+        for h in range(2):
+            keys[h] = rotated(projected[0, :, h * HD : (h + 1) * HD])
+            values[h] = projected[1, :, h * HD : (h + 1) * HD].astype(jnp.bfloat16)
 
     def attend(step):
         q_chunk = step - 2
@@ -480,7 +511,31 @@
         pass_on(step - 3)
         return carry
 
-    lax.fori_loop(3, SLOTS, project_second, 0)
+    def project_none(step, carry):
+        attend(step - 1)
+        finished(step, projected[step])
+        pass_on(step - 3)
+        return carry
+
+    @pl.when(p == 0)
+    def _():
+        lax.fori_loop(EARLY, SLOTS, first_half, 0)
+        row_scales()
+        scaled_whole.wait_recv()
+        lax.fori_loop(0, 3, second_half, 0)
+        keys_and_values()
+        lax.fori_loop(3, SLOTS, project_second, 0)
+
+    @pl.when(p == 1)
+    def _():
+        for step in range(SLOTS, CHUNKS):
+            weight_copy(step).start()
+        row_scales()
+        for step in range(3):
+            finished(step, projected[step])
+        keys_and_values()
+        lax.fori_loop(3, SLOTS, project_none, 0)
+
     lax.fori_loop(SLOTS, CHUNKS, project_both, 0)
     attend(CHUNKS - 1)
     inject(PIECES - 1)
@@ -504,13 +559,6 @@
             c_r.at[p, place_of(e), zz],
             device(stream_of(e), pipe=1),
         )
-
-    def nth(j):
-        pair, odd = j // 2, j % 2
-        along = (pair * (3 - pair)) // 2
-        dy = along * (3 + 2 * odd) + 2 * (pair // 3)
-        dx = (1 - along) * odd + (pair // 2) * (1 - pair // 3)
-        return at(y + dy, (xl + dx) % 2)
 
     def unit(e, zb):
         stream, xb = stream_of(e), xl + p * (e % 2 - xl)

time: 113 us -> 111 us (0.982)
    pallas_call x1, Pallas kernels: 110 us -> 109 us  [local(): pl.pallas_call(kernel, out_shape=jax.ShapeDtypeStruct((SEQ, HALF), bf16),...]
where the time goes in v5:
time: 111 us
  Pallas kernels  109 us (98%)
  local copies, waits for them, and re-layouts  2.29 us (2%)
    pallas_call x1, Pallas kernels, local(): pl.pallas_call(kernel, out_shape=jax.ShapeDtypeStruct((SEQ, HALF), bf16),...  109 us
    unnamed x1, local copies, waits for them, and re-layouts  2.29 us

profile of v5, /device:TPU:7, one launch (start us, length us, event | category | flops | bytes accessed | tf_op | source)
XLA Modules:
  0.0 111.2 jit_solution(15332649929767482271)
XLA Ops:
  0.0 108.9 %sublayers.1 = bf16[128,4096]{1,0:T(8,128)(2,1)} custom-call(bf16[128,4096]{1,0:T(8,128)(2,1)} %bitcast.6, f32[1,8192]{1,0:T(1,128)} %gain_in.1, bf16[8192,2560]{1,0:T(8,128)(2,1)} %bitcast.4, f32[1,2560]{1,0:T(1,128)} %bias_in.1, bf16[2048,256]{1,0:T(8,128)(2,1)} %bitcast.7, s32[1,128]{1,0:T(1,128)} %seg_in.1, s32[1,2]{1,0:T(1,128)} %start_in.1, ...), custom_call_target="tpu_custom_call" | custom-call | tf_op jit(solution)/shard_map/sublayers/pallas_call | solution.py:749
  108.9 2.3 %copy.12 = bf16[1,1,128,4096]{3,2,1,0:T(8,128)(2,1)} copy(bf16[1,1,128,4096]{3,2,1,0:T(8,128)(2,1)} %bitcast.5) | data formatting | bytes 2097152

commit v6 on v5

--- a/solution.py
+++ b/solution.py
@@ -16,6 +16,7 @@
 CHUNKS = 10
 SLOTS = 8
 EARLY = 1
+LAG = 2
 AHEAD = 2
 PIECES = 4
 PIECE = 512
@@ -604,6 +605,30 @@
 
         lax.fori_loop(0, 8, body, 0)
 
+    def staggered(count, entry):
+        def body(i, carry):
+            @pl.when(i < count)
+            def _():
+                unit(*entry(i))
+
+            @pl.when(i >= LAG)
+            def _():
+                finish(*entry(i - LAG))
+
+            return carry
+
+        lax.fori_loop(0, count + LAG, body, 0)
+
+    def staggered_each(count, place):
+        def entry(i):
+            j, turn = place(i)
+            return nth(j), (z + turn) % 4
+
+        staggered(count, entry)
+
+    def staggered_along(dy):
+        staggered(8, lambda i: (at(y + dy, (xl + i // 4) % 2), (z + i % 4) % 4))
+
     def near(i):
         return i, 0
 
@@ -644,21 +669,17 @@
         for k in range(PIECES):
             weight_pass_up(k).wait_recv()
             weight_pass_down(k).wait_recv()
-        each(unit, 4, far)
-        each(finish, 4, far)
+        staggered_each(4, far)
         pass_second(2)
         pass_second(3)
         for k in range(PIECES):
             rows_copy(k, 3).wait_recv()
             rows_copy(k, 4).wait_recv()
-        each(unit, 8, corner)
-        each(finish, 8, corner)
-        each(unit, 4, facing)
-        each(finish, 4, facing)
+        staggered_each(8, corner)
+        staggered_each(4, facing)
         for k in range(PIECES):
             rows_copy(k, 7).wait_recv()
-        each(unit, 4, last)
-        each(finish, 4, last)
+        staggered_each(4, last)
 
     @pl.when(p == 1)
     def _():
@@ -671,15 +692,12 @@
         each_along(unit, 0)
         pass_along(2)
         pass_along(3)
-        each_along(unit, 3)
-        each_along(finish, 3)
-        each_along(unit, 1)
-        each_along(finish, 1)
+        staggered_along(3)
+        staggered_along(1)
         for k in range(PIECES):
             rows_copy(k, 5).wait_recv()
             rows_copy(k, 6).wait_recv()
-        each_along(unit, 2)
-        each_along(finish, 2)
+        staggered_along(2)
         each_along(finish, 0)
 
     @pl.when(p == 0)

time: 111 us -> 111 us (level)
  no operation moved by 1% of the time
where the time goes in v6:
time: 111 us
  Pallas kernels  109 us (98%)
  local copies, waits for them, and re-layouts  2.29 us (2%)
    pallas_call x1, Pallas kernels, local(): pl.pallas_call(kernel, out_shape=jax.ShapeDtypeStruct((SEQ, HALF), bf16),...  109 us
    unnamed x1, local copies, waits for them, and re-layouts  2.29 us

profile of v6, /device:TPU:7, one launch (start us, length us, event | category | flops | bytes accessed | tf_op | source)
XLA Modules:
  0.0 110.9 jit_solution(9466406593451831032)
XLA Ops:
  0.0 108.6 %sublayers.1 = bf16[128,4096]{1,0:T(8,128)(2,1)} custom-call(bf16[128,4096]{1,0:T(8,128)(2,1)} %bitcast.6, f32[1,8192]{1,0:T(1,128)} %gain_in.1, bf16[8192,2560]{1,0:T(8,128)(2,1)} %bitcast.4, f32[1,2560]{1,0:T(1,128)} %bias_in.1, bf16[2048,256]{1,0:T(8,128)(2,1)} %bitcast.7, s32[1,128]{1,0:T(1,128)} %seg_in.1, s32[1,2]{1,0:T(1,128)} %start_in.1, ...), custom_call_target="tpu_custom_call" | custom-call | tf_op jit(solution)/shard_map/sublayers/pallas_call | solution.py:767
  108.6 2.3 %copy.12 = bf16[1,1,128,4096]{3,2,1,0:T(8,128)(2,1)} copy(bf16[1,1,128,4096]{3,2,1,0:T(8,128)(2,1)} %bitcast.5) | data formatting | bytes 2097152
